TPU v7x, 128 devices: a whole 4x4x4 slice. The times are simulated.
128 devices in a mesh: row: 4 (over y), col: 32 (over z, x, core).
Axes of the slice: x: 4, y: 4, z: 4, core: 2. Of those that a mesh axis runs over, the one named last changes fastest.
Arguments:
- boundary: bfloat16 [32, 4, 128, 8, 128], P('col'), may hold values from -6 to 6
- peps_rows: bfloat16 [4, 32, 8, 8, 8, 8], P('row', 'col'), may hold values from -2 to 2
- sketch: bfloat16 [4, 32, 4, 1024, 128], P('row', 'col'), may hold values from -0.1875 to 0.1875
- ranks: int32 [4, 32, 4], P('row', 'col'), may hold values from 64 to 128
- sizes: int32 [4], replicated, may hold values from 64 to 128
- charges: int32 [8], replicated, may hold values from -1 to 1
Outputs:
- absorbed: bfloat16 [4, 32, 4, 128, 8, 128], P('row', 'col')
All inputs are finite; a program needn't handle non-finite values.
Results may differ from a plain program's by a relative error of at most 0.03.
Values may be sent and summed in bfloat16 or wider, within the bound.
A program may use at most 128 MiB of HBM per device.

v0:
```python
from functools import partial

import jax
import jax.numpy as jnp
from jax import lax
from jax.sharding import PartitionSpec as P


def as_sent(shard):

    def short(part):
        return part.astype(jnp.bfloat16) if part.dtype == jnp.float32 else part

    return jax.tree.map(short, shard)


def passed_along(shard, axis, by):
    peers = lax.axis_size(axis)
    return lax.ppermute(shard, axis, [(i, (i + by) % peers) for i in range(peers)])


def shifted(shard, axis, by):
    peers = lax.axis_size(axis)
    pairs = [(i, i + by) for i in range(peers) if 0 <= i + by < peers]
    return lax.ppermute(shard, axis, pairs)


def sketch_column(blocks, tensor, right_sketch, left_sketch):
    wide = jnp.float32
    bond_sketch = jnp.einsum(
        "saub,sbrk->saurk", blocks, right_sketch, preferred_element_type=wide
    ).astype(jnp.bfloat16)
    left_side = jnp.einsum(
        "saurk,lrud->saldk", bond_sketch, tensor, preferred_element_type=wide
    ).astype(jnp.bfloat16)
    edge_sketch = jnp.einsum(
        "salk,saub->sklub", left_sketch, blocks, preferred_element_type=wide
    ).astype(jnp.bfloat16)
    right_side = jnp.einsum(
        "sklub,lrud->skdrb", edge_sketch, tensor, preferred_element_type=wide
    ).astype(jnp.bfloat16)
    gram_left = jnp.einsum("saldk,saldm->skm", left_side, left_side, preferred_element_type=wide)
    gram_right = jnp.einsum("skdrb,smdrb->skm", right_side, right_side, preferred_element_type=wide)
    middle = jnp.einsum("salk,saldm->skdm", left_sketch, left_side, preferred_element_type=wide)
    return (gram_left, gram_right, middle)


def finish_column(middle, left_factor, right_factor):
    sectors, tile_width, bond_depth, _ = middle.shape
    solver = jax.vmap(partial(jax.scipy.linalg.solve_triangular, lower=True))
    flattened = middle.reshape(sectors, tile_width, bond_depth * tile_width)
    lefted = solver(left_factor, flattened).reshape(sectors, tile_width, bond_depth, tile_width)
    turned = jnp.transpose(lefted, (0, 3, 1, 2)).reshape(
        sectors, tile_width, tile_width * bond_depth
    )
    righted = solver(right_factor, turned).reshape(sectors, tile_width, tile_width, bond_depth)
    result = jnp.transpose(righted, (0, 2, 3, 1))
    scaling = lax.rsqrt(jnp.mean(result * result, axis=(1, 2, 3), keepdims=True) + 1e-06)
    return (result * scaling).astype(jnp.bfloat16)


def absorb(blocks, tensors, right_sketch, left_sketch, active):
    column_count, sector_count, tile_width, bond_depth, _ = blocks.shape

    def measure():
        return jax.vmap(sketch_column)(blocks, tensors, right_sketch, left_sketch)

    def nothing():
        zero_gram = jnp.zeros((column_count, sector_count, tile_width, tile_width), jnp.float32)
        zero_middle = jnp.zeros(
            (column_count, sector_count, tile_width, bond_depth, tile_width), jnp.float32
        )
        return (zero_gram, zero_gram, zero_middle)

    grams_left, grams_right, middles = lax.cond(active, measure, nothing)
    from_left = passed_along(as_sent(grams_left[-1]), "col", 1)
    from_right = passed_along(as_sent(grams_right[0]), "col", -1)
    identity = jnp.eye(tile_width, dtype=jnp.float32)
    later = jnp.concatenate([grams_right[1:], from_right[None]], axis=0)
    first_bond = from_left + grams_right[0] + identity
    bond_matrices = jnp.concatenate([first_bond[None], grams_left + later + identity], axis=0)
    factors = jnp.linalg.cholesky(bond_matrices)

    def settle():
        return jax.vmap(finish_column)(middles, factors[:-1], factors[1:])

    def unchanged():
        return blocks

    return lax.cond(active, settle, unchanged)


def body(boundary, peps_rows, sketch, ranks, sizes, charges):
    row_rank = lax.axis_index("row")
    section_count = lax.axis_size("row")
    column_count, sector_count, tile_width, bond_depth, _ = boundary.shape
    row_count = peps_rows.shape[0]
    positions = jnp.arange(tile_width, dtype=jnp.int32)
    inside = (positions[None, :] < sizes[:, None]).astype(boundary.dtype)
    blocks = boundary * inside[None, :, :, None, None] * inside[None, :, None, None, :]
    conserved = (
        charges[:, None, None, None] + charges[None, None, :, None]
        == charges[None, :, None, None] + charges[None, None, None, :]
    )
    tensors = jnp.where(conserved[None, None], peps_rows, jnp.zeros_like(peps_rows))
    kept_mask = (positions[None, None, None, :] < ranks[:, :, :, None]).astype(sketch.dtype)
    right_all = (
        sketch.reshape(row_count, column_count, sector_count, tile_width, bond_depth, tile_width)
        * kept_mask[:, :, :, None, None, :]
    )
    from_left = passed_along(right_all[:, -1], "col", 1)
    left_all = jnp.concatenate([from_left[:, None], right_all[:, :-1]], axis=1)
    carried = blocks
    for section_turn in range(section_count):
        portion = carried
        right_sketch = right_all[0]
        left_sketch = left_all[0]
        portion = absorb(portion, tensors[0], right_sketch, left_sketch, row_rank == section_turn)
        carried = portion
        if section_turn + 1 < section_count:
            incoming = jax.tree.map(
                lambda part, own: part.astype(own.dtype),
                shifted(as_sent(carried), "row", 1),
                carried,
            )
            carried = jnp.where(row_rank == section_turn + 1, incoming, carried)
    return carried[None]


def solution(mesh):
    placed = (
        P("col", None, None, None, None),
        P("row", "col", None, None, None, None),
        P("row", "col", None, None, None),
        P("row", "col", None),
        P(),
        P(),
    )
    return jax.shard_map(
        body,
        mesh=mesh,
        in_specs=placed,
        out_specs=P("row", "col", None, None, None, None),
        check_vma=False,
    )
```

profile of v0, /device:TPU:24, one launch (start us, length us, event | category | flops | bytes accessed | tf_op | source)
XLA Modules:
  0.0 1222.0 jit_solution(12981296484126536108)
XLA Ops:
  0.7 2.3 bitcast_multiply_fusion.8
  3.0 1.0 copy.269
  4.8 0.8 broadcast_add_fusion
  5.6 0.7 fusion.200
  6.3 1.7 multiply_multiply_fusion
  8.1 13.3 %collective-permute-done = bf16[1,4,128,8,128]{4,3,2,1,0:T(8,128)(2,1)S(1)} collective-permute-done((bf16[1,4,128,8,128]{4,3,2,1,0:T(8,128)(2,1)}, bf16[1,4,128,8,128]{4,3,2,1,0:T(8,128)(2,1)S(1)}, u32[]{:S(2)}, u32[]{:S(2)}) %collective-permute-start) | collective-permute-done | bytes 1048608 | tf_op jit(solution)/shard_map/ppermute | solution.py:19
  21.4 6.2 conditional.8
  21.4 1.6 broadcast.232
  27.8 2.5 collective-permute-done.2
  30.5 7.8 collective-permute-done.1
  38.3 0.8 pad_maximum_fusion
  39.1 2.0 copy.276
  41.2 1.9 fusion.187
  43.1 95.3 %custom-call.24 = f32[2,4,128,128]{3,2,1,0:T(8,128)} custom-call(f32[2,4,128,128]{3,2,1,0:T(8,128)} %fusion.187), custom_call_target="Cholesky" | custom-call | tf_op jit(solution)/shard_map/jit(cholesky)/cholesky | solution.py:82
  138.6 1.3 collective-permute-start.3
  139.9 19.3 %collective-permute-done.3 = bf16[1,4,128,8,128]{4,3,2,1,0:T(8,128)(2,1)} collective-permute-done((bf16[1,4,128,8,128]{4,3,2,1,0:T(8,128)(2,1)S(1)}, bf16[1,4,128,8,128]{4,3,2,1,0:T(8,128)(2,1)}, u32[]{:S(2)}, u32[]{:S(2)}) %collective-permute-start.3) | collective-permute-done | bytes 1048608 | tf_op jit(solution)/shard_map/ppermute | solution.py:25
  159.2 1.1 broadcast_select_fusion
  160.3 6.1 conditional.10
  160.3 1.6 broadcast.236
  167.3 5.7 collective-permute-start.5
  173.0 2.5 collective-permute-done.5
  175.5 1.1 convert_bitcast_fusion.6
  176.7 7.8 collective-permute-done.4
  184.6 0.8 pad_maximum_fusion.1
  185.4 2.0 copy.284
  187.5 1.9 fusion.186
  189.4 94.6 %custom-call.25 = f32[2,4,128,128]{3,2,1,0:T(8,128)S(1)} custom-call(f32[2,4,128,128]{3,2,1,0:T(8,128)} %fusion.186), custom_call_target="Cholesky" | custom-call | tf_op jit(solution)/shard_map/jit(cholesky)/cholesky | solution.py:82
  284.1 1.3 collective-permute-start.6
  285.4 19.5 %collective-permute-done.6 = bf16[1,4,128,8,128]{4,3,2,1,0:T(8,128)(2,1)} collective-permute-done((bf16[1,4,128,8,128]{4,3,2,1,0:T(8,128)(2,1)}, bf16[1,4,128,8,128]{4,3,2,1,0:T(8,128)(2,1)}, u32[]{:S(2)}, u32[]{:S(2)}) %collective-permute-start.6) | collective-permute-done | bytes 1048608 | tf_op jit(solution)/shard_map/ppermute | solution.py:25
  304.9 1.3 broadcast_select_fusion.1
  306.3 6.8 conditional.12
  306.3 1.6 broadcast.240
  313.7 1.1 copy.290
  314.9 6.0 collective-permute-start.8
  320.8 2.5 collective-permute-done.8
  323.3 1.1 convert_bitcast_fusion.5
  324.5 7.8 collective-permute-done.7
  333.1 0.8 pad_maximum_fusion.2
  333.9 2.0 copy.292
  336.0 2.0 fusion.185
  338.0 95.3 %custom-call.26 = f32[2,4,128,128]{3,2,1,0:T(8,128)} custom-call(f32[2,4,128,128]{3,2,1,0:T(8,128)} %fusion.185), custom_call_target="Cholesky" | custom-call | tf_op jit(solution)/shard_map/jit(cholesky)/cholesky | solution.py:82
  433.4 1.3 collective-permute-start.9
  434.7 507.1 %collective-permute-done.9 = bf16[1,4,128,8,128]{4,3,2,1,0:T(8,128)(2,1)} collective-permute-done((bf16[1,4,128,8,128]{4,3,2,1,0:T(8,128)(2,1)S(1)}, bf16[1,4,128,8,128]{4,3,2,1,0:T(8,128)(2,1)}, u32[]{:S(2)}, u32[]{:S(2)}) %collective-permute-start.9) | collective-permute-done | bytes 1048608 | tf_op jit(solution)/shard_map/ppermute | solution.py:25
  941.8 2.3 broadcast_select_fusion.2
  944.1 79.2 %conditional.14 = (f32[1,4,128,128]{3,2,1,0:T(8,128)S(1)}, f32[1,4,128,8,128]{2,4,3,1,0:T(8,128)}, f32[1,4,128,128]{2,3,1,0:T(8,128)S(1)}) conditional(s32[]{:T(128)} %convert_element_type.308, () %tuple.74, (bf16[1,4,128,8,128]{4,3,2,1,0:T(8,128)(2,1)}, bf16[1,4,128,8,128]{4,3,2,1,0:T(8,128)(2,1)}, bf16[1,8,8,8,8]{3,4,1,2,0:T(8,128)(2,1)}, ...), branch_computations={%region_17.20_spmd, %region_18.21_spmd} | conditional | flops 6459228160 | bytes 89669688 | solution.py:75
  944.3 1.8 copy.294
  946.1 5.6 convert_bitcast_fusion.3
  951.7 12.1 copy.349
  963.7 8.3 fusion.116
  972.0 23.6 %fusion.128 = f32[1,4,128,128]{3,2,1,0:T(8,128)S(1)} fusion(bf16[4,128,8,8,128]{4,2,3,1,0:T(8,128)(2,1)} %fusion.116), kind=kOutput, calls=%fused_computation.97 | convolution fusion | flops 1073741824 | bytes 8650752 | tf_op jit(solution)/shard_map/cond/branch_1_fun/vmap(skdrb,smdrb->skm)/dot_general | solution.py:43
  995.6 7.9 fusion.117
  1003.5 11.3 fusion.120
  1014.8 8.3 fusion.125
  1024.2 5.4 collective-permute-start.11
  1029.6 2.5 collective-permute-done.11
  1032.1 1.1 convert_bitcast_fusion.4
  1033.3 7.8 collective-permute-done.10
  1041.5 93.8 %custom-call.27 = f32[2,4,128,128]{3,2,1,0:T(8,128)S(1)} custom-call(f32[2,4,128,128]{3,2,1,0:T(8,128)S(1)} %fusion.184), custom_call_target="Cholesky" | custom-call | tf_op jit(solution)/shard_map/jit(cholesky)/cholesky | solution.py:82
  1135.2 86.5 %conditional.15 = (bf16[1,1,4,128,8,128]{5,4,3,2,1,0:T(8,128)(2,1)}) conditional(s32[]{:T(128)} %convert_element_type.308, bf16[1,4,128,8,128]{4,3,2,1,0:T(8,128)(2,1)} %broadcast_select_fusion.2, (pred[128,128]{1,0:T(8,128)(4,1)S(1)}, f32[1,4,128,8,128]{2,4,3,1,0:T(8,128)}, pred[128,128]{1,0:T(8,128)(4,1)S(1)}, ...), branch_computations={%region_19.22_spmd, %region_20.24_spmd.clone} | conditional | flops 1613382656 | bytes 20521052 | solution.py:90
  1135.9 39.3 %custom-call.34 = f32[1,4,1,128,128]{3,4,2,1,0:T(8,128)S(1)} custom-call(f32[1,4,1,128,128]{4,3,2,1,0:T(8,128)S(1)} %get-tuple-element.375), custom_call_target="InvertDiagBlocksLowerTriangular" | custom-call | tf_op jit(solution)/shard_map/cond/branch_1_fun/vmap(vmap(jit(_solve_triangular)))/triangular_solve | solution.py:52
  1175.2 3.5 fusion.181
  1179.2 39.3 %custom-call.35 = f32[1,4,1,128,128]{3,4,2,1,0:T(8,128)S(1)} custom-call(f32[1,4,1,128,128]{4,3,2,1,0:T(8,128)S(1)} %get-tuple-element.374), custom_call_target="InvertDiagBlocksLowerTriangular" | custom-call | tf_op jit(solution)/shard_map/cond/branch_1_fun/vmap(vmap(jit(_solve_triangular)))/triangular_solve | solution.py:56
  1218.6 2.0 fusion.174
  1220.6 1.2 fusion.178
  (55 shorter events, 7.9 us)
Async XLA Ops:
  3.0 18.4 %collective-permute-start = (bf16[1,4,128,8,128]{4,3,2,1,0:T(8,128)(2,1)}, bf16[1,4,128,8,128]{4,3,2,1,0:T(8,128)(2,1)S(1)}, u32[]{:S(2)}, u32[]{:S(2)}) collective-permute-start(bf16[1,4,128,8,128]{4,3,2,1,0:T(8,128)(2,1)} %bitcast_multiply_fusion.8), channel_id=1, source_target_pairs={{0,1},{1,2},{2,3},{3,4},{4,5},{5,6},{6,7},{7,8},{8,9},{9,10},{10,1... | collective-permute-start | bytes 3145736 | tf_op jit(solution)/shard_map/ppermute | solution.py:19
  27.7 2.6 collective-permute-start.2
  30.3 7.9 collective-permute-start.1
  138.6 20.6 %collective-permute-start.3 = (bf16[1,4,128,8,128]{4,3,2,1,0:T(8,128)(2,1)S(1)}, bf16[1,4,128,8,128]{4,3,2,1,0:T(8,128)(2,1)}, u32[]{:S(2)}, u32[]{:S(2)}) collective-permute-start(bf16[1,4,128,8,128]{4,3,2,1,0:T(8,128)(2,1)S(1)} %get-tuple-element.414), channel_id=1, source_target_pairs={{0,32},{32,64},{64,96},{1,33},{33,65},{65,97},{2,34},{34,66},{66,9... | collective-permute-start | bytes 3145736 | tf_op jit(solution)/shard_map/ppermute | solution.py:25
  166.4 0.7 copy-start.4
  167.3 8.2 collective-permute-start.5
  176.7 7.9 collective-permute-start.4
  284.1 20.8 %collective-permute-start.6 = (bf16[1,4,128,8,128]{4,3,2,1,0:T(8,128)(2,1)}, bf16[1,4,128,8,128]{4,3,2,1,0:T(8,128)(2,1)}, u32[]{:S(2)}, u32[]{:S(2)}) collective-permute-start(bf16[1,4,128,8,128]{4,3,2,1,0:T(8,128)(2,1)} %get-tuple-element.415), channel_id=1, source_target_pairs={{0,32},{32,64},{64,96},{1,33},{33,65},{65,97},{2,34},{34,66},{66,9... | collective-permute-start | bytes 3145736 | tf_op jit(solution)/shard_map/ppermute | solution.py:25
  313.0 0.7 copy-start.5
  314.9 8.5 collective-permute-start.8
  324.4 8.0 copy-start.2
  324.4 7.9 collective-permute-start.7
  332.4 0.7 copy-start.3
  433.4 508.4 %collective-permute-start.9 = (bf16[1,4,128,8,128]{4,3,2,1,0:T(8,128)(2,1)S(1)}, bf16[1,4,128,8,128]{4,3,2,1,0:T(8,128)(2,1)}, u32[]{:S(2)}, u32[]{:S(2)}) collective-permute-start(bf16[1,4,128,8,128]{4,3,2,1,0:T(8,128)(2,1)S(1)} %get-tuple-element.416), channel_id=1, source_target_pairs={{0,32},{32,64},{64,96},{1,33},{33,65},{65,97},{2,34},{34,66},{66,9... | collective-permute-start | bytes 3145736 | tf_op jit(solution)/shard_map/ppermute | solution.py:25
  972.0 23.6 %copy-start.1 = (bf16[1,4,128,8,128]{4,3,2,1,0:T(8,128)(2,1)S(1)}, bf16[1,4,128,8,128]{4,3,2,1,0:T(8,128)(2,1)}, u32[]{:S(2)}) copy-start(bf16[1,4,128,8,128]{4,3,2,1,0:T(8,128)(2,1)} %get-tuple-element.212) | copy-start | bytes 3145732 | tf_op jit(solution)/shard_map/cond
  1023.3 0.7 copy-start.6
  1024.2 7.9 collective-permute-start.11
  1033.2 7.9 collective-permute-start.10
where the time goes:
time: 1230 us; the launch traced here: 1220 us
  waiting for transfers between devices  600 us (49%)
  other arithmetic  483 us (39%)
  matrix products  70.4 us (6%)
  local copies, waits for them, and re-layouts  31.6 us (3%)
  starting transfers between devices  21.4 us (2%)
  loops' own time  14.7 us (1%)
    ppermute x3, waiting for transfers between devices, shifted(): return lax.ppermute(shard, axis, pairs)  546 us
    another operation x7, other arithmetic, absorb(): factors = jnp.linalg.cholesky(bond_matrices)  379 us
    ppermute x9, waiting for transfers between devices, passed_along(): lax.ppermute(shard, axis, [(i, (i + by) % peers) for i in range(peers)])  54.7 us
    another operation x3, other arithmetic, finish_column(): solver(right_factor, turned)  39.4 us
    another operation x1, other arithmetic, finish_column(): solver(left_factor, flattened)  39.3 us
  transfers between devices with their start and end apart: 12, of which 12 were waited for; matrix products, arithmetic and copies ran while one was open for 0% of the time, Pallas kernels for 0%

commit v1 on v0

v1 whole, which is shorter than its diff:
```python
import functools

import jax
import jax.numpy as jnp
from jax import lax
from jax.experimental import pallas as pl
from jax.experimental.pallas import tpu as pltpu
from jax.sharding import PartitionSpec as P

W = 128
D = 8
NS = 4
F32 = jnp.float32
BF16 = jnp.bfloat16
TOP = lax.Precision.HIGHEST
MESH = pl.DeviceIdType.MESH


def iota(shape, axis):
    return lax.broadcasted_iota(jnp.int32, shape, axis)


def mm(a, b, precision=None):
    return jnp.dot(a, b, preferred_element_type=F32, precision=precision)


def mm_nt(a, b, precision=None):
    return lax.dot_general(
        a, b, (((1,), (1,)), ((), ())), preferred_element_type=F32, precision=precision
    )


def mm_tn(a, b, precision=None):
    return lax.dot_general(
        a, b, (((0,), (0,)), ((), ())), preferred_element_type=F32, precision=precision
    )


def compact_tensor(peps_ref, charges_ref, compact):
    rows = iota((512, 1), 0)
    l, h, u = rows >> 6, (rows >> 3) & 7, rows & 7
    balance = jnp.zeros((512, 1), jnp.int32)
    for i in range(D):
        q = charges_ref[i]
        balance += q * (
            (l == i).astype(jnp.int32) + (u == i).astype(jnp.int32) - (h == i).astype(jnp.int32)
        )
    values = peps_ref[...].astype(F32).reshape(512, D)
    big = iota((512, 256), 0)
    lane = iota((512, 256), 1) & 63
    same_hu = (big & 63) == lane
    same_lu = (((big >> 6) << 3) | (big & 7)) == lane
    pick = iota((D, 512), 0)
    from_row = iota((D, 512), 1)
    pick_l = (pick == (from_row >> 6)).astype(BF16)
    pick_h = (pick == ((from_row >> 3) & 7)).astype(BF16)
    for d in range(D):
        column = jnp.where(balance == charges_ref[d], values[:, d : d + 1], 0.0)
        spread = jnp.broadcast_to(column, (512, 256))
        compact[0, pl.ds(d * D, D), :] = mm(pick_l, jnp.where(same_hu, spread, 0.0).astype(BF16))
        compact[1, pl.ds(d * D, D), :] = mm(pick_h, jnp.where(same_lu, spread, 0.0).astype(BF16))


def inverse_factors(work, inverse):
    row = iota((8, 256), 0)
    lane = iota((8, 256), 1)
    for p in range(W // 8):
        for i in range(2):
            panel = work[i, pl.ds(8 * p, 8), :]
            for t in range(7):
                j = 8 * p + t
                column = panel[:, j : j + 1]
                factor = column / panel[t : t + 1, j : j + 1]
                panel = panel - jnp.where(row > t, factor, 0.0) * panel[t : t + 1, :]
            pivots = jnp.sum(jnp.where(lane == row + 8 * p, panel, 0.0), axis=1, keepdims=True)
            panel = panel * lax.rsqrt(pivots)
            inverse[i, pl.ds(8 * p, 8), :] = panel[:, W:]
            if p < W // 8 - 1:
                update = mm_tn(panel[:, :W], panel, TOP)
                work[i, pl.ds(8 * p + 8, W - 8 * p - 8), :] -= update[8 * p + 8 :, :]


def kernel(
    peps_ref, ranks_ref, sizes_ref, charges_ref, boundary_ref, sketch_ref, out_ref,
    sk, bm, bt, r_raw, l_raw, r_wide, l_wide, l_turned, comp32, comp, kron, z, z2, mid, tall,
    gram_own, gl_out, gr_out, gl_in, gr_in, work, inverse,
    sk_sem, b_sem, r_send, r_recv, w_send, w_recv, l_send, l_recv,
    gl_send, gl_recv, gr_send, gr_recv, o_send, o_recv, o_local,
):
    me = lax.axis_index("row")
    col = lax.axis_index("col")
    cols = lax.axis_size("col")
    right = lax.rem(col + 1, cols)
    left = lax.rem(col + cols - 1, cols)

    def sketch_load(s):
        return pltpu.make_async_copy(sketch_ref.at[s], sk.at[s], sk_sem.at[s])

    for s in range(NS):
        sketch_load(s).start()
    boundary_load = pltpu.make_async_copy(boundary_ref.at[me], bm.at[0], b_sem)
    boundary_load.start()

    barrier = pltpu.get_barrier_semaphore()
    for k in range(1, NS):
        pl.semaphore_signal(
            barrier, inc=1, device_id=(lax.rem(me + k, NS), col), device_id_type=MESH
        )
    for c in (left, right):
        pl.semaphore_signal(barrier, inc=1, device_id=(me, c), device_id_type=MESH)
    pl.semaphore_wait(barrier, NS + 1)

    lanes = iota((1, W), 1)
    for s in range(NS):
        sketch_load(s).wait()
        kept = (lanes < ranks_ref[s]).astype(BF16)
        sk[s] = sk[s] * kept
    r_raw[me] = sk[me]

    def r_copy(k):
        s = lax.rem(me + k, NS)
        return pltpu.make_async_remote_copy(
            src_ref=sk.at[s], dst_ref=r_raw.at[me], send_sem=r_send.at[k - 1],
            recv_sem=r_recv.at[me], device_id=(s, col), device_id_type=MESH,
        )

    def r_arrival(r):
        return pltpu.make_async_remote_copy(
            src_ref=sk.at[0], dst_ref=r_raw.at[r], send_sem=r_send.at[0],
            recv_sem=r_recv.at[r], device_id=(me, col), device_id_type=MESH,
        )

    def w_copy(k):
        s = lax.rem(me + k, NS)
        return pltpu.make_async_remote_copy(
            src_ref=comp.at[me], dst_ref=comp.at[me], send_sem=w_send.at[k - 1],
            recv_sem=w_recv.at[me], device_id=(s, col), device_id_type=MESH,
        )

    def w_arrival(r):
        return pltpu.make_async_remote_copy(
            src_ref=comp.at[r], dst_ref=comp.at[r], send_sem=w_send.at[0],
            recv_sem=w_recv.at[r], device_id=(me, col), device_id_type=MESH,
        )

    def l_copy(r):
        return pltpu.make_async_remote_copy(
            src_ref=r_raw.at[r], dst_ref=l_raw.at[r], send_sem=l_send.at[r],
            recv_sem=l_recv.at[r], device_id=(me, right), device_id_type=MESH,
        )

    def gl_copy(r):
        return pltpu.make_async_remote_copy(
            src_ref=gl_out.at[r], dst_ref=gl_in.at[r], send_sem=gl_send.at[r],
            recv_sem=gl_recv.at[r], device_id=(me, right), device_id_type=MESH,
        )

    def gr_copy(r):
        return pltpu.make_async_remote_copy(
            src_ref=gr_out.at[r], dst_ref=gr_in.at[r], send_sem=gr_send.at[r],
            recv_sem=gr_recv.at[r], device_id=(me, left), device_id_type=MESH,
        )

    def o_copy(r):
        return pltpu.make_async_remote_copy(
            src_ref=bm.at[r + 1], dst_ref=out_ref.at[me], send_sem=o_send.at[r],
            recv_sem=o_recv.at[me], device_id=(r, col), device_id_type=MESH,
        )

    def o_arrival(s):
        return pltpu.make_async_remote_copy(
            src_ref=bm.at[1], dst_ref=out_ref.at[s], send_sem=o_send.at[0],
            recv_sem=o_recv.at[s], device_id=(me, col), device_id_type=MESH,
        )

    def o_stay(r):
        return pltpu.make_async_copy(bm.at[r + 1], out_ref.at[me], o_local)

    @pl.when(me == 0)
    def _():
        for k in (2, 1, 3):
            r_copy(k).start()

    compact_tensor(peps_ref, charges_ref, comp32)
    comp[me] = comp32[...].astype(BF16)
    for k in range(1, NS):
        w_copy(k).start()

    size = sizes_ref[me]
    boundary_load.wait()
    start = jnp.where(
        ((iota((W * D, W), 0) >> 3) < size) & (iota((W * D, W), 1) < size),
        bm[0].astype(F32), 0.0,
    )
    bm[0] = start.astype(BF16)
    tall[...] = start
    for u in range(D):
        mid[:, u * W : (u + 1) * W] = tall[pl.ds(u, W, stride=D), :].T
    for u in range(D):
        tall[pl.ds(u, W, stride=D), :] = mid[:, u * W : (u + 1) * W]
    bt[...] = tall[...].astype(BF16)

    block = iota((256, 256), 0) >> 6 == iota((256, 256), 1) >> 6

    def prepare(r):
        @pl.when(r != me)
        def _():
            r_arrival(r).wait_recv()

        l_copy(r).start()

        @pl.when((r == 0) & (me != 0))
        def _():
            for k in (2, 1, 3):
                r_copy(k).start()

        tall[...] = r_raw[r].astype(F32)
        for h in range(D):
            r_wide[:, h * W : (h + 1) * W] = tall[pl.ds(h, W, stride=D), :].astype(BF16)

        @pl.when(r != me)
        def _():
            w_arrival(r).wait_recv()

        for i in range(2):
            one = comp[r, i]
            kron[i] = jnp.where(block, jnp.concatenate([one] * 4, axis=0).astype(F32), 0.0).astype(
                BF16
            )
        l_copy(r).wait_recv()
        natural = l_raw[r].astype(F32)
        tall[...] = natural
        for h in range(D):
            l_wide[:, h * W : (h + 1) * W] = tall[pl.ds(h, W, stride=D), :].astype(BF16)
        l_turned[...] = natural.T.astype(BF16)

    def sided(lhs, wide, tensor, store):
        for g in range(W // 16):
            part = mm(lhs[pl.ds(g * 128, 128), :], wide)
            columns = []
            for q in range(4):
                pieces = [
                    part[(4 * q + i) * D : (4 * q + i + 1) * D, h * W : (h + 1) * W]
                    for i in range(4)
                    for h in range(D)
                ]
                columns.append(jnp.concatenate(pieces, axis=0).astype(BF16))
            side = mm(tensor, jnp.concatenate(columns, axis=1))
            store(g, side)

    def store_left(g, side):
        for d in range(D):
            pieces = [
                side[(i * D + d) * D : (i * D + d + 1) * D, q * W : (q + 1) * W]
                for q in range(4)
                for i in range(4)
            ]
            z[pl.ds(g * 128, 128), d * W : (d + 1) * W] = jnp.concatenate(pieces, axis=0).astype(
                BF16
            )

    def store_right(g, side):
        z2[g] = side.astype(BF16)

    prepare(0)

    def absorb(r, carry):
        sided(bm.at[r], r_wide[...], kron[0], store_left)
        gram = jnp.zeros((W, W), F32)
        for d in range(D):
            piece = z[:, d * W : (d + 1) * W]
            gram += mm_tn(piece, piece)
        gram_own[0] = gram
        gl_out[r] = gram.astype(BF16)
        gl_copy(r).start()
        sided(bt, l_wide[...], kron[1], store_right)
        gram = jnp.zeros((W, W), F32)
        for g in range(W // 16):
            for q in range(4):
                piece = z2[g, :, q * W : (q + 1) * W]
                gram += mm_tn(piece, piece)
        gram_own[1] = gram
        gr_out[r] = gram.astype(BF16)
        gr_copy(r).start()
        mid[...] = mm(l_turned[...], z[...])

        @pl.when(r < NS - 1)
        def _():
            prepare(r + 1)

        eye = (iota((W, W), 0) == iota((W, W), 1)).astype(F32)
        gl_copy(r).wait_recv()
        gr_copy(r).wait_recv()
        work[0, :, :W] = gl_in[r].astype(F32) + gram_own[1] + eye
        work[1, :, :W] = gr_in[r].astype(F32) + gram_own[0] + eye
        work[0, :, W:] = eye
        work[1, :, W:] = eye
        inverse_factors(work, inverse)
        lefted = mm(inverse[0], mid[...], TOP)
        for d in range(D):
            tall[pl.ds(d, W, stride=D), :] = lefted[:, d * W : (d + 1) * W]
        fresh = mm_nt(tall[...], inverse[1], TOP)
        scaling = lax.rsqrt(jnp.mean(fresh * fresh) + 1e-6)
        bm[r + 1] = (fresh * scaling).astype(BF16)

        @pl.when(r != me)
        def _():
            o_copy(r).start()

        @pl.when(r == me)
        def _():
            o_stay(r).start()

        @pl.when(r < NS - 1)
        def _():
            for d in range(D):
                tall[pl.ds(d, W, stride=D), :] = mm_nt(
                    inverse[1], lefted[:, d * W : (d + 1) * W], TOP
                )
            bt[...] = (tall[...] * scaling).astype(BF16)

        return carry

    lax.fori_loop(0, NS, absorb, 0)

    for k in range(1, NS):
        r_copy(k).wait_send()
        w_copy(k).wait_send()
    for r in range(NS):
        l_copy(r).wait_send()
        gl_copy(r).wait_send()
        gr_copy(r).wait_send()
    for r in range(NS):

        @pl.when(r != me)
        def _():
            o_copy(r).wait_send()
            o_arrival(r).wait_recv()

    o_stay(me).wait()


def body(boundary, peps_rows, sketch, ranks, sizes, charges):
    any_space = pl.BlockSpec(memory_space=pl.ANY)
    smem = pl.BlockSpec(memory_space=pltpu.SMEM)
    vmem = pl.BlockSpec(memory_space=pltpu.VMEM)
    dma = pltpu.SemaphoreType.DMA
    result = pl.pallas_call(
        kernel,
        out_shape=jax.ShapeDtypeStruct((NS, W * D, W), BF16),
        in_specs=[vmem, smem, smem, smem, any_space, any_space],
        out_specs=any_space,
        scratch_shapes=[
            pltpu.VMEM((NS, W * D, W), BF16),
            pltpu.VMEM((NS + 1, W * D, W), BF16),
            pltpu.VMEM((W * D, W), BF16),
            pltpu.VMEM((NS, W * D, W), BF16),
            pltpu.VMEM((NS, W * D, W), BF16),
            pltpu.VMEM((W, W * D), BF16),
            pltpu.VMEM((W, W * D), BF16),
            pltpu.VMEM((W, W * D), BF16),
            pltpu.VMEM((2, 64, 256), F32),
            pltpu.VMEM((NS, 2, 64, 256), BF16),
            pltpu.VMEM((2, 256, 256), BF16),
            pltpu.VMEM((W * D, W * D), BF16),
            pltpu.VMEM((W // 16, 256, 4 * W), BF16),
            pltpu.VMEM((W, W * D), F32),
            pltpu.VMEM((W * D, W), F32),
            pltpu.VMEM((2, W, W), F32),
            pltpu.VMEM((NS, W, W), BF16),
            pltpu.VMEM((NS, W, W), BF16),
            pltpu.VMEM((NS, W, W), BF16),
            pltpu.VMEM((NS, W, W), BF16),
            pltpu.VMEM((2, W, 2 * W), F32),
            pltpu.VMEM((2, W, W), F32),
            dma((NS,)), dma(()), dma((NS - 1,)), dma((NS,)), dma((NS - 1,)), dma((NS,)),
            dma((NS,)), dma((NS,)), dma((NS,)), dma((NS,)), dma((NS,)), dma((NS,)),
            dma((NS,)), dma((NS,)), dma(()),
        ],
        compiler_params=pltpu.CompilerParams(
            collective_id=0, has_side_effects=True, vmem_limit_bytes=56 * 2**20
        ),
        name="absorb_rows",
    )(
        peps_rows.reshape(D * D, D, D),
        ranks.reshape(NS),
        sizes,
        charges,
        boundary.reshape(NS, W * D, W),
        sketch.reshape(NS, W * D, W),
    )
    return result.reshape(1, 1, NS, W, D, W)


def solution(mesh):
    placed = (
        P("col", None, None, None, None),
        P("row", "col", None, None, None, None),
        P("row", "col", None, None, None),
        P("row", "col", None),
        P(),
        P(),
    )
    return jax.shard_map(
        body,
        mesh=mesh,
        in_specs=placed,
        out_specs=P("row", "col", None, None, None, None),
        check_vma=False,
    )
```

time: 1230 us -> 156 us (0.13)
  waiting for transfers between devices: 600 us -> 0 us
  other arithmetic: 483 us -> 0 us
  Pallas kernels: 0 us -> 153 us
  matrix products: 70.4 us -> 0 us
  local copies, waits for them, and re-layouts: 31.6 us -> 2.26 us
  starting transfers between devices: 21.4 us -> 0 us
  loops' own time: 14.7 us -> 0 us
    ppermute x12 -> x0, waiting for transfers between devices: 600 us -> none  [the longest x3 546 us: shifted(): return lax.ppermute(shard, axis, pairs)]
    another operation x11 -> x0, other arithmetic: 458 us -> none  [the longest x7 379 us: absorb(): factors = jnp.linalg.cholesky(bond_matrices)]
    pallas_call x0 -> x1, Pallas kernels: none -> 153 us  [body(): pl.pallas_call(kernel, out_shape=jax.ShapeDtypeStruct((NS, W * D, W), BF1...]
    dot_general x6 -> x0, matrix products: 64.9 us -> none  [the longest x1 23.6 us: sketch_column(): jnp.einsum('skdrb,smdrb->skm', right_side, right_side, preferred_element_...]
    ppermute x12 -> x0, starting transfers between devices: 21.4 us -> none  [the longest x9 17.5 us: passed_along(): lax.ppermute(shard, axis, [(i, (i + by) % peers) for i in range(peers)])]
    another operation x13 -> x0, local copies, waits for them, and re-layouts: 19.5 us -> none
    another operation x8 -> x0, loops' own time: 14.7 us -> none  [the longest x4 13.8 us: absorb(): grams_left, grams_right, middles = lax.cond(active, measure, nothing)]
  transfers between devices with their start and end apart: 12 -> 0, of which waited for: 12 -> 0; matrix products, arithmetic and copies ran while one was open for 0% -> 0% of each run, Pallas kernels for 0% -> 0%
where the time goes in v1:
time: 156 us; the launch traced here: 155 us
  Pallas kernels  153 us (98%)
  local copies, waits for them, and re-layouts  2.26 us (1%)
    pallas_call x1, Pallas kernels, body(): pl.pallas_call(kernel, out_shape=jax.ShapeDtypeStruct((NS, W * D, W), BF1...  153 us

profile of v1, /device:TPU:24, one launch (start us, length us, event | category | flops | bytes accessed | tf_op | source)
XLA Modules:
  0.0 155.4 jit_solution(11188042469241556488)
XLA Ops:
  0.0 153.2 %absorb_rows.1 = bf16[4,1024,128]{2,1,0:T(8,128)(2,1)} custom-call(bf16[64,8,8]{2,1,0:T(8,128)(2,1)} %bitcast.8, s32[4]{0:T(128)} %bitcast.9, s32[4]{0:T(128)} %sizes_ref.1, s32[8]{0:T(128)} %charges_ref.1, bf16[4,1024,128]{2,1,0:T(8,128)(2,1)} %bitcast.6, bf16[4,1024,128]{2,1,0:T(8,128)(2,1)} %bitcast.7), custom_call_target="tpu_custom_call" | custom-call | tf_op jit(solution)/shard_map/absorb_rows/pallas_call | solution.py:348
  153.2 2.3 %copy.8 = bf16[1,1,4,128,8,128]{5,4,3,2,1,0:T(8,128)(2,1)} copy(bf16[1,1,4,128,8,128]{5,4,3,2,1,0:T(8,128)(2,1)} %bitcast.5) | data formatting | bytes 2097152

commit v2 on v1

--- a/solution.py
+++ b/solution.py
@@ -1,5 +1,3 @@
-import functools
-
 import jax
 import jax.numpy as jnp
 from jax import lax
@@ -12,7 +10,6 @@
 NS = 4
 F32 = jnp.float32
 BF16 = jnp.bfloat16
-TOP = lax.Precision.HIGHEST
 MESH = pl.DeviceIdType.MESH
 
 
@@ -20,20 +17,16 @@
     return lax.broadcasted_iota(jnp.int32, shape, axis)
 
 
-def mm(a, b, precision=None):
-    return jnp.dot(a, b, preferred_element_type=F32, precision=precision)
-
-
-def mm_nt(a, b, precision=None):
-    return lax.dot_general(
-        a, b, (((1,), (1,)), ((), ())), preferred_element_type=F32, precision=precision
-    )
-
-
-def mm_tn(a, b, precision=None):
-    return lax.dot_general(
-        a, b, (((0,), (0,)), ((), ())), preferred_element_type=F32, precision=precision
-    )
+def mm(a, b):
+    return jnp.dot(a, b, preferred_element_type=F32)
+
+
+def mm_nt(a, b):
+    return lax.dot_general(a, b, (((1,), (1,)), ((), ())), preferred_element_type=F32)
+
+
+def mm_tn(a, b):
+    return lax.dot_general(a, b, (((0,), (0,)), ((), ())), preferred_element_type=F32)
 
 
 def compact_tensor(peps_ref, charges_ref, compact):
@@ -61,29 +54,109 @@
         compact[1, pl.ds(d * D, D), :] = mm(pick_h, jnp.where(same_lu, spread, 0.0).astype(BF16))
 
 
-def inverse_factors(work, inverse):
-    row = iota((8, 256), 0)
-    lane = iota((8, 256), 1)
-    for p in range(W // 8):
+def halves(x):
+    high = x.astype(BF16)
+    return high, (x - high.astype(F32)).astype(BF16)
+
+
+def mm3(a, b):
+    ah, al = halves(a)
+    bh, bl = halves(b)
+    return mm(jnp.concatenate([ah, ah, al], axis=1), jnp.concatenate([bh, bl, bh], axis=0))
+
+
+def mm3_tn(a, b):
+    ah, al = halves(a)
+    bh, bl = halves(b)
+    return mm_tn(jnp.concatenate([ah, ah, al], axis=0), jnp.concatenate([bh, bl, bh], axis=0))
+
+
+def vreg(x):
+    return jnp.broadcast_to(x, (8, W))
+
+
+def eliminate(tiles, first, part):
+    sub = iota((8, W), 0)
+    tiles = list(tiles)
+
+    def spread(v, j):
+        a, b = (first[0] + j) % W, (first[1] + j) % W
+        return jnp.where(part, vreg(v[:, a : a + 1]), vreg(v[:, b : b + 1]))
+
+    for q in range(4):
+        columns = [spread(tiles[q], 8 * q + t) for t in range(8)]
+        s = {(i, t): vreg(columns[t][i : i + 1, :]) for t in range(8) for i in range(t, 8)}
+        low = {o: [spread(tiles[o], 8 * q + t) for t in range(8)] for o in range(q + 1, 4)}
+        f, n, root = {}, {}, []
+        for t in range(8):
+            root.append(lax.rsqrt(s[t, t]))
+            over = root[t] * root[t]
+            for i in range(t + 1, 8):
+                f[i, t] = s[i, t] * over
+                for k in range(t + 1, i + 1):
+                    s[i, k] = s[i, k] - (s[i, t] * s[k, t]) * over
+        for j in range(8):
+            for i in range(j + 1, 8):
+                total = f[i, j]
+                for k in range(j + 1, i):
+                    total = total + f[i, k] * n[k, j]
+                n[i, j] = -total
+        g = {
+            (i, j): (root[i] if i == j else n[i, j] * root[i])
+            for j in range(8)
+            for i in range(j, 8)
+        }
+        panel, result = tiles[q], None
+        for j in range(8):
+            column = jnp.zeros((8, W), F32)
+            for i in range(j, 8):
+                column = jnp.where(sub == i, g[i, j], column)
+            term = column * vreg(panel[j : j + 1, :])
+            result = term if result is None else result + term
+        tiles[q] = result
+        for o in range(q + 1, 4):
+            rest = tiles[o]
+            for t in range(8):
+                factor = None
+                for j in range(t + 1):
+                    term = low[o][j] * g[t, j]
+                    factor = term if factor is None else factor + term
+                rest = rest - factor * vreg(result[t : t + 1, :])
+            tiles[o] = rest
+    return tiles
+
+
+def inverse_factors(work, inverse, mixed):
+    lane, sub = iota((8, W), 1), iota((8, W), 0)
+    group = lane >> 5
+    for k in range(4):
+        at = [(k + i) % 4 for i in range(4)]
+        part = (group == at[0]) | (group == at[1])
+        tiles = []
+        for q in range(4):
+            rows = pl.ds(32 * k + 8 * q, 8)
+            one = work[0, rows, :W]
+            two = pltpu.roll(work[1, rows, :W], 64, 1)
+            unit = ((lane & 31) == (sub + 8 * q)).astype(F32)
+            tiles.append(jnp.where(group == at[0], one, jnp.where(group == at[2], two, unit)))
+        done = jnp.concatenate(eliminate(tiles, (32 * k, 32 * k + 64), part), axis=0)
+        mixed[...] = jnp.zeros((W, 4 * W), F32)
+        mixed[pl.ds(32 * at[1], 32), : 2 * W] = work[0, pl.ds(32 * k, 32), :]
+        mixed[pl.ds(32 * at[3], 32), 2 * W :] = work[1, pl.ds(32 * k, 32), :]
+        both = mm3(done, mixed[...])
         for i in range(2):
-            panel = work[i, pl.ds(8 * p, 8), :]
-            for t in range(7):
-                j = 8 * p + t
-                column = panel[:, j : j + 1]
-                factor = column / panel[t : t + 1, j : j + 1]
-                panel = panel - jnp.where(row > t, factor, 0.0) * panel[t : t + 1, :]
-            pivots = jnp.sum(jnp.where(lane == row + 8 * p, panel, 0.0), axis=1, keepdims=True)
-            panel = panel * lax.rsqrt(pivots)
-            inverse[i, pl.ds(8 * p, 8), :] = panel[:, W:]
-            if p < W // 8 - 1:
-                update = mm_tn(panel[:, :W], panel, TOP)
-                work[i, pl.ds(8 * p + 8, W - 8 * p - 8), :] -= update[8 * p + 8 :, :]
+            panel = both[:, i * 2 * W : (i + 1) * 2 * W]
+            inverse[i, pl.ds(32 * k, 32), :] = panel[:, W:]
+            if k < 3:
+                below = 32 * (k + 1)
+                update = mm3_tn(panel[:, :W], panel)
+                work[i, pl.ds(below, W - below), :] -= update[below:, :]
 
 
 def kernel(
     peps_ref, ranks_ref, sizes_ref, charges_ref, boundary_ref, sketch_ref, out_ref,
     sk, bm, bt, r_raw, l_raw, r_wide, l_wide, l_turned, comp32, comp, kron, z, z2, mid, tall,
-    gram_own, gl_out, gr_out, gl_in, gr_in, work, inverse,
+    gram_own, gl_out, gr_out, gl_in, gr_in, work, inverse, mixed,
     sk_sem, b_sem, r_send, r_recv, w_send, w_recv, l_send, l_recv,
     gl_send, gl_recv, gr_send, gr_recv, o_send, o_recv, o_local,
 ):
@@ -202,7 +275,7 @@
 
     block = iota((256, 256), 0) >> 6 == iota((256, 256), 1) >> 6
 
-    def prepare(r):
+    def prepare_right(r):
         @pl.when(r != me)
         def _():
             r_arrival(r).wait_recv()
@@ -227,6 +300,8 @@
             kron[i] = jnp.where(block, jnp.concatenate([one] * 4, axis=0).astype(F32), 0.0).astype(
                 BF16
             )
+
+    def prepare_left(r):
         l_copy(r).wait_recv()
         natural = l_raw[r].astype(F32)
         tall[...] = natural
@@ -234,38 +309,29 @@
             l_wide[:, h * W : (h + 1) * W] = tall[pl.ds(h, W, stride=D), :].astype(BF16)
         l_turned[...] = natural.T.astype(BF16)
 
-    def sided(lhs, wide, tensor, store):
-        for g in range(W // 16):
-            part = mm(lhs[pl.ds(g * 128, 128), :], wide)
-            columns = []
-            for q in range(4):
-                pieces = [
-                    part[(4 * q + i) * D : (4 * q + i + 1) * D, h * W : (h + 1) * W]
-                    for i in range(4)
-                    for h in range(D)
-                ]
-                columns.append(jnp.concatenate(pieces, axis=0).astype(BF16))
-            side = mm(tensor, jnp.concatenate(columns, axis=1))
-            store(g, side)
-
-    def store_left(g, side):
+    def sided(lhs, wide, tensor):
+        part = mm(lhs, wide)
+        columns = []
+        for q in range(W // 4):
+            pieces = [
+                part[(4 * q + i) * D : (4 * q + i + 1) * D, h * W : (h + 1) * W]
+                for i in range(4)
+                for h in range(D)
+            ]
+            columns.append(jnp.concatenate(pieces, axis=0).astype(BF16))
+        return mm(tensor, jnp.concatenate(columns, axis=1))
+
+    prepare_right(0)
+
+    def absorb(r, carry):
+        side = sided(bm[r], r_wide[...], kron[0])
         for d in range(D):
             pieces = [
                 side[(i * D + d) * D : (i * D + d + 1) * D, q * W : (q + 1) * W]
-                for q in range(4)
+                for q in range(W // 4)
                 for i in range(4)
             ]
-            z[pl.ds(g * 128, 128), d * W : (d + 1) * W] = jnp.concatenate(pieces, axis=0).astype(
-                BF16
-            )
-
-    def store_right(g, side):
-        z2[g] = side.astype(BF16)
-
-    prepare(0)
-
-    def absorb(r, carry):
-        sided(bm.at[r], r_wide[...], kron[0], store_left)
+            z[:, d * W : (d + 1) * W] = jnp.concatenate(pieces, axis=0).astype(BF16)
         gram = jnp.zeros((W, W), F32)
         for d in range(D):
             piece = z[:, d * W : (d + 1) * W]
@@ -273,12 +339,15 @@
         gram_own[0] = gram
         gl_out[r] = gram.astype(BF16)
         gl_copy(r).start()
-        sided(bt, l_wide[...], kron[1], store_right)
-        gram = jnp.zeros((W, W), F32)
-        for g in range(W // 16):
-            for q in range(4):
-                piece = z2[g, :, q * W : (q + 1) * W]
-                gram += mm_tn(piece, piece)
+
+        @pl.when(r == 0)
+        def _():
+            prepare_left(0)
+
+        side = sided(bt[...], l_wide[...], kron[1]).astype(BF16)
+        for q in range(W // 4):
+            z2[pl.ds(q * 256, 256), :] = side[:, q * W : (q + 1) * W]
+        gram = mm_tn(z2[...], z2[...])
         gram_own[1] = gram
         gr_out[r] = gram.astype(BF16)
         gr_copy(r).start()
@@ -286,7 +355,8 @@
 
         @pl.when(r < NS - 1)
         def _():
-            prepare(r + 1)
+            prepare_right(r + 1)
+            prepare_left(r + 1)
 
         eye = (iota((W, W), 0) == iota((W, W), 1)).astype(F32)
         gl_copy(r).wait_recv()
@@ -295,11 +365,14 @@
         work[1, :, :W] = gr_in[r].astype(F32) + gram_own[0] + eye
         work[0, :, W:] = eye
         work[1, :, W:] = eye
-        inverse_factors(work, inverse)
-        lefted = mm(inverse[0], mid[...], TOP)
+        inverse_factors(work, inverse, mixed)
+        lefted = mm3(inverse[0], mid[...])
         for d in range(D):
             tall[pl.ds(d, W, stride=D), :] = lefted[:, d * W : (d + 1) * W]
-        fresh = mm_nt(tall[...], inverse[1], TOP)
+        high, low = halves(inverse[1])
+        second = jnp.concatenate([high, low, high], axis=1)
+        high, low = halves(tall[...])
+        fresh = mm_nt(jnp.concatenate([high, high, low], axis=1), second)
         scaling = lax.rsqrt(jnp.mean(fresh * fresh) + 1e-6)
         bm[r + 1] = (fresh * scaling).astype(BF16)
 
@@ -313,10 +386,11 @@
 
         @pl.when(r < NS - 1)
         def _():
+            high, low = halves(lefted)
             for d in range(D):
-                tall[pl.ds(d, W, stride=D), :] = mm_nt(
-                    inverse[1], lefted[:, d * W : (d + 1) * W], TOP
-                )
+                lanes_d = slice(d * W, (d + 1) * W)
+                piece = jnp.concatenate([high[:, lanes_d], high[:, lanes_d], low[:, lanes_d]], axis=1)
+                tall[pl.ds(d, W, stride=D), :] = mm_nt(second, piece)
             bt[...] = (tall[...] * scaling).astype(BF16)
 
         return carry
@@ -363,7 +437,7 @@
             pltpu.VMEM((NS, 2, 64, 256), BF16),
             pltpu.VMEM((2, 256, 256), BF16),
             pltpu.VMEM((W * D, W * D), BF16),
-            pltpu.VMEM((W // 16, 256, 4 * W), BF16),
+            pltpu.VMEM((W // 4 * 256, W), BF16),
             pltpu.VMEM((W, W * D), F32),
             pltpu.VMEM((W * D, W), F32),
             pltpu.VMEM((2, W, W), F32),
@@ -373,6 +447,7 @@
             pltpu.VMEM((NS, W, W), BF16),
             pltpu.VMEM((2, W, 2 * W), F32),
             pltpu.VMEM((2, W, W), F32),
+            pltpu.VMEM((W, 4 * W), F32),
             dma((NS,)), dma(()), dma((NS - 1,)), dma((NS,)), dma((NS - 1,)), dma((NS,)),
             dma((NS,)), dma((NS,)), dma((NS,)), dma((NS,)), dma((NS,)), dma((NS,)),
             dma((NS,)), dma((NS,)), dma(()),

time: 156 us -> 94.7 us (0.61)
  Pallas kernels: 153 us -> 92 us
    pallas_call x1, Pallas kernels: 153 us -> 92 us  [body(): pl.pallas_call(kernel, out_shape=jax.ShapeDtypeStruct((NS, W * D, W), BF1...]
where the time goes in v2:
time: 94.7 us; the launch traced here: 94.3 us
  Pallas kernels  92 us (97%)
  local copies, waits for them, and re-layouts  2.26 us (2%)
    pallas_call x1, Pallas kernels, body(): pl.pallas_call(kernel, out_shape=jax.ShapeDtypeStruct((NS, W * D, W), BF1...  92 us
    unnamed x1, local copies, waits for them, and re-layouts  2.26 us

profile of v2, /device:TPU:24, one launch (start us, length us, event | category | flops | bytes accessed | tf_op | source)
XLA Modules:
  0.0 94.3 jit_solution(531238843791255304)
XLA Ops:
  0.0 92.0 %absorb_rows.1 = bf16[4,1024,128]{2,1,0:T(8,128)(2,1)} custom-call(bf16[64,8,8]{2,1,0:T(8,128)(2,1)} %bitcast.8, s32[4]{0:T(128)} %bitcast.9, s32[4]{0:T(128)} %sizes_ref.1, s32[8]{0:T(128)} %charges_ref.1, bf16[4,1024,128]{2,1,0:T(8,128)(2,1)} %bitcast.6, bf16[4,1024,128]{2,1,0:T(8,128)(2,1)} %bitcast.7), custom_call_target="tpu_custom_call" | custom-call | tf_op jit(solution)/shard_map/absorb_rows/pallas_call | solution.py:422
  92.1 2.3 %copy.8 = bf16[1,1,4,128,8,128]{5,4,3,2,1,0:T(8,128)(2,1)} copy(bf16[1,1,4,128,8,128]{5,4,3,2,1,0:T(8,128)(2,1)} %bitcast.5) | data formatting | bytes 2097152

commit v3 on v2

v3 whole, which is shorter than its diff:
```python
import jax
import jax.numpy as jnp
from jax import lax
from jax.experimental import pallas as pl
from jax.experimental.pallas import tpu as pltpu
from jax.sharding import PartitionSpec as P

W = 128
D = 8
NS = 4
CHUNKS = 4
CHUNK = W * D // CHUNKS
F32 = jnp.float32
BF16 = jnp.bfloat16
MESH = pl.DeviceIdType.MESH


def iota(shape, axis):
    return lax.broadcasted_iota(jnp.int32, shape, axis)


def mm(a, b):
    return jnp.dot(a, b, preferred_element_type=F32)


def mm_nt(a, b):
    return lax.dot_general(a, b, (((1,), (1,)), ((), ())), preferred_element_type=F32)


def mm_tn(a, b):
    return lax.dot_general(a, b, (((0,), (0,)), ((), ())), preferred_element_type=F32)


def compact_tensor(peps_ref, charges_ref, compact):
    rows = iota((512, 1), 0)
    l, h, u = rows >> 6, (rows >> 3) & 7, rows & 7
    balance = jnp.zeros((512, 1), jnp.int32)
    for i in range(D):
        q = charges_ref[i]
        balance += q * (
            (l == i).astype(jnp.int32) + (u == i).astype(jnp.int32) - (h == i).astype(jnp.int32)
        )
    values = peps_ref[...].astype(F32).reshape(512, D)
    big = iota((512, W), 0)
    lane = iota((512, W), 1)
    from_row = jnp.where(lane < 64, big & 63, ((big >> 6) << 3) | (big & 7))
    same = from_row == (lane & 63)
    pick = iota((2 * D, 512), 0)
    source = iota((2 * D, 512), 1)
    wanted = jnp.where(pick < D, source >> 6, (source >> 3) & 7)
    picker = (wanted == (pick & 7)).astype(BF16)
    for d in range(D):
        column = jnp.where(balance == charges_ref[d], values[:, d : d + 1], 0.0)
        spread = jnp.where(same, jnp.broadcast_to(column, (512, W)), 0.0).astype(BF16)
        both = mm(picker, spread)
        compact[pl.ds(d * D, D), :] = jnp.where(iota((D, W), 1) < 64, both[:D], both[D:])


def halves(x):
    high = x.astype(BF16)
    return high, (x - high.astype(F32)).astype(BF16)


def mm3(a, b):
    ah, al = halves(a)
    bh, bl = halves(b)
    return mm(jnp.concatenate([ah, ah, al], axis=1), jnp.concatenate([bh, bl, bh], axis=0))


def mm3_tn(a, b):
    ah, al = halves(a)
    bh, bl = halves(b)
    return mm_tn(jnp.concatenate([ah, ah, al], axis=0), jnp.concatenate([bh, bl, bh], axis=0))


def vreg(x):
    return jnp.broadcast_to(x, (8, W))


def eliminate(tiles, first, part):
    sub = iota((8, W), 0)
    tiles = list(tiles)

    def spread(v, j):
        a, b = (first[0] + j) % W, (first[1] + j) % W
        return jnp.where(part, vreg(v[:, a : a + 1]), vreg(v[:, b : b + 1]))

    for q in range(4):
        columns = [spread(tiles[q], 8 * q + t) for t in range(8)]
        s = {(i, t): vreg(columns[t][i : i + 1, :]) for t in range(8) for i in range(t, 8)}
        low = {o: [spread(tiles[o], 8 * q + t) for t in range(8)] for o in range(q + 1, 4)}
        f, n, root = {}, {}, []
        for t in range(8):
            root.append(lax.rsqrt(s[t, t]))
            over = root[t] * root[t]
            for i in range(t + 1, 8):
                f[i, t] = s[i, t] * over
                for k in range(t + 1, i + 1):
                    s[i, k] = s[i, k] - (s[i, t] * s[k, t]) * over
        for j in range(8):
            for i in range(j + 1, 8):
                total = f[i, j]
                for k in range(j + 1, i):
                    total = total + f[i, k] * n[k, j]
                n[i, j] = -total
        g = {
            (i, j): (root[i] if i == j else n[i, j] * root[i])
            for j in range(8)
            for i in range(j, 8)
        }
        panel, result = tiles[q], None
        for j in range(8):
            column = jnp.zeros((8, W), F32)
            for i in range(j, 8):
                column = jnp.where(sub == i, g[i, j], column)
            term = column * vreg(panel[j : j + 1, :])
            result = term if result is None else result + term
        tiles[q] = result
        for o in range(q + 1, 4):
            rest = tiles[o]
            for t in range(8):
                factor = None
                for j in range(t + 1):
                    term = low[o][j] * g[t, j]
                    factor = term if factor is None else factor + term
                rest = rest - factor * vreg(result[t : t + 1, :])
            tiles[o] = rest
    return tiles


def inverse_factors(work, inverse, mixed):
    lane, sub = iota((8, W), 1), iota((8, W), 0)
    group = lane >> 5
    for k in range(4):
        at = [(k + i) % 4 for i in range(4)]
        part = (group == at[0]) | (group == at[1])
        tiles = []
        for q in range(4):
            rows = pl.ds(32 * k + 8 * q, 8)
            one = work[0, rows, :W]
            two = pltpu.roll(work[1, rows, :W], 64, 1)
            unit = ((lane & 31) == (sub + 8 * q)).astype(F32)
            tiles.append(jnp.where(group == at[0], one, jnp.where(group == at[2], two, unit)))
        done = jnp.concatenate(eliminate(tiles, (32 * k, 32 * k + 64), part), axis=0)
        mixed[...] = jnp.zeros((W, 4 * W), F32)
        mixed[pl.ds(32 * at[1], 32), : 2 * W] = work[0, pl.ds(32 * k, 32), :]
        mixed[pl.ds(32 * at[3], 32), 2 * W :] = work[1, pl.ds(32 * k, 32), :]
        both = mm3(done, mixed[...])
        for i in range(2):
            panel = both[:, i * 2 * W : (i + 1) * 2 * W]
            inverse[i, pl.ds(32 * k, 32), :] = panel[:, W:]
            if k < 3:
                below = 32 * (k + 1)
                update = mm3_tn(panel[:, :W], panel)
                work[i, pl.ds(below, W - below), :] -= update[below:, :]


def kernel(
    peps_ref, ranks_ref, sizes_ref, charges_ref, boundary_ref, sketch_ref, out_ref,
    sk, bm, sides, r_raw, l_raw, wides, l_turned, comp32, comp, kron, z, mid, tall,
    gram_own, gram_out, gram_in, work, inverse, mixed,
    sk_sem, b_sem, r_send, r_recv, w_send, w_recv, l_send, l_recv,
    g_send, g_recv, o_send, o_recv, o_local,
):
    me = lax.axis_index("row")
    col = lax.axis_index("col")
    cols = lax.axis_size("col")
    right = lax.rem(col + 1, cols)
    left = lax.rem(col + cols - 1, cols)

    def sketch_load(s):
        return pltpu.make_async_copy(sketch_ref.at[s], sk.at[s], sk_sem.at[s])

    def chunk(c):
        return pl.ds(c * CHUNK, CHUNK)

    def r_copy(k, c):
        s = lax.rem(me + k, NS)
        return pltpu.make_async_remote_copy(
            src_ref=sk.at[s, chunk(c)], dst_ref=r_raw.at[me, chunk(c)],
            send_sem=r_send.at[k - 1, c], recv_sem=r_recv.at[me, c],
            device_id=(s, col), device_id_type=MESH,
        )

    def r_arrival(r, c):
        return pltpu.make_async_remote_copy(
            src_ref=sk.at[0, chunk(c)], dst_ref=r_raw.at[r, chunk(c)],
            send_sem=r_send.at[0, c], recv_sem=r_recv.at[r, c],
            device_id=(me, col), device_id_type=MESH,
        )

    def l_copy(r, c):
        return pltpu.make_async_remote_copy(
            src_ref=r_raw.at[r, chunk(c)], dst_ref=l_raw.at[r, chunk(c)],
            send_sem=l_send.at[r, c], recv_sem=l_recv.at[r, c],
            device_id=(me, right), device_id_type=MESH,
        )

    def w_copy(k):
        s = lax.rem(me + k, NS)
        return pltpu.make_async_remote_copy(
            src_ref=comp.at[me], dst_ref=comp.at[me], send_sem=w_send.at[k - 1],
            recv_sem=w_recv.at[me], device_id=(s, col), device_id_type=MESH,
        )

    def w_arrival(r):
        return pltpu.make_async_remote_copy(
            src_ref=comp.at[r], dst_ref=comp.at[r], send_sem=w_send.at[0],
            recv_sem=w_recv.at[r], device_id=(me, col), device_id_type=MESH,
        )

    def g_copy(r, side):
        return pltpu.make_async_remote_copy(
            src_ref=gram_out.at[r, side], dst_ref=gram_in.at[r, side],
            send_sem=g_send.at[r, side], recv_sem=g_recv.at[r, side],
            device_id=(me, right + side * (left - right)), device_id_type=MESH,
        )

    def o_copy(r):
        return pltpu.make_async_remote_copy(
            src_ref=bm.at[r + 1], dst_ref=out_ref.at[me], send_sem=o_send.at[r],
            recv_sem=o_recv.at[me], device_id=(r, col), device_id_type=MESH,
        )

    def o_arrival(s):
        return pltpu.make_async_remote_copy(
            src_ref=bm.at[1], dst_ref=out_ref.at[s], send_sem=o_send.at[0],
            recv_sem=o_recv.at[s], device_id=(me, col), device_id_type=MESH,
        )

    def o_stay(r):
        return pltpu.make_async_copy(bm.at[r + 1], out_ref.at[me], o_local)

    def send_sketch(k):
        for c in range(CHUNKS):
            r_copy(k, c).start()

    barrier = pltpu.get_barrier_semaphore()
    for k in range(1, NS):
        pl.semaphore_signal(
            barrier, inc=1, device_id=(lax.rem(me + k, NS), col), device_id_type=MESH
        )
    for c in (left, right):
        pl.semaphore_signal(barrier, inc=1, device_id=(me, c), device_id_type=MESH)
    for s in range(NS):
        sketch_load(s).start()
    boundary_load = pltpu.make_async_copy(boundary_ref.at[me], bm.at[0], b_sem)
    boundary_load.start()
    lanes = iota((1, W), 1)
    for s in range(NS):
        sketch_load(s).wait()
        sk[s] = sk[s] * (lanes < ranks_ref[s]).astype(BF16)
    r_raw[me] = sk[me]
    pl.semaphore_wait(barrier, NS + 1)

    @pl.when(me == 0)
    def _():
        send_sketch(1)
        send_sketch(3)

    @pl.when(me == 1)
    def _():
        send_sketch(3)

    @pl.when(me == 2)
    def _():
        send_sketch(1)
        send_sketch(3)
        send_sketch(2)

    compact_tensor(peps_ref, charges_ref, comp32)
    comp[me] = comp32[...].astype(BF16)
    for k in range(1, NS):
        w_copy(k).start()

    block = iota((256, 256), 0) >> 6 == iota((256, 256), 1) >> 6

    def relay(r):
        for c in range(CHUNKS):

            @pl.when(r != me)
            def _():
                r_arrival(r, c).wait_recv()

            l_copy(r, c).start()

        @pl.when(r != me)
        def _():
            w_arrival(r).wait_recv()

    def regroup(side, natural):
        tall[...] = natural
        for h in range(D):
            wides[side, :, h * W : (h + 1) * W] = tall[pl.ds(h, W, stride=D), :].astype(BF16)

    def prepare_right(r):
        regroup(0, r_raw[r].astype(F32))
        both = comp[r].astype(F32)
        turned = pltpu.roll(both, 64, 1)
        low = iota((64, W), 1) < 64
        for i, (one, two) in enumerate(((both, turned), (turned, both))):
            twice = jnp.where(low, one, two)
            four = jnp.concatenate([twice, twice], axis=1)
            kron[i] = jnp.where(block, jnp.concatenate([four] * 4, axis=0), 0.0).astype(BF16)

    def prepare_left(r):
        natural = l_raw[r].astype(F32)
        regroup(1, natural)
        l_turned[...] = natural.T.astype(BF16)

    def left_arrives(r):
        for c in range(CHUNKS):
            l_copy(r, c).wait_recv()

    def absorb_side(r, side):
        part = mm(sides[side], wides[side])
        columns = []
        for q in range(W // 4):
            pieces = [
                part[(4 * q + i) * D : (4 * q + i + 1) * D, h * W : (h + 1) * W]
                for i in range(4)
                for h in range(D)
            ]
            columns.append(jnp.concatenate(pieces, axis=0).astype(BF16))
        whole = mm(kron[side], jnp.concatenate(columns, axis=1))
        for d in range(D):
            pieces = [
                whole[(i * D + d) * D : (i * D + d + 1) * D, q * W : (q + 1) * W]
                for q in range(W // 4)
                for i in range(4)
            ]
            z[side, :, d * W : (d + 1) * W] = jnp.concatenate(pieces, axis=0).astype(BF16)
        gram = jnp.zeros((W, W), F32)
        for d in range(D):
            piece = z[side, :, d * W : (d + 1) * W]
            gram += mm_tn(piece, piece)
        gram_own[side] = gram
        gram_out[r, side] = gram.astype(BF16)
        g_copy(r, side).start()

    @pl.when(me == 0)
    def _():
        for c in range(CHUNKS):
            r_copy(1, c).wait_send()
        send_sketch(2)

    size = sizes_ref[me]
    boundary_load.wait()
    start = jnp.where(
        ((iota((W * D, W), 0) >> 3) < size) & (iota((W * D, W), 1) < size),
        bm[0].astype(F32), 0.0,
    )
    sides[0] = start.astype(BF16)
    tall[...] = start
    for u in range(D):
        mid[:, u * W : (u + 1) * W] = tall[pl.ds(u, W, stride=D), :].T
    for u in range(D):
        tall[pl.ds(u, W, stride=D), :] = mid[:, u * W : (u + 1) * W]
    sides[1] = tall[...].astype(BF16)

    relay(0)
    prepare_right(0)
    eye = (iota((W, W), 0) == iota((W, W), 1)).astype(F32)

    def absorb(r, carry):
        early = jnp.where(r == 0, 0, 1 - lax.rem(col, 2))
        absorb_side(r, early)

        @pl.when(r == 0)
        def _():
            left_arrives(0)

            @pl.when(me == 1)
            def _():
                send_sketch(1)

            prepare_left(0)

        absorb_side(r, 1 - early)
        mid[...] = mm(l_turned[...], z[0])

        @pl.when((r == 0) & (me == 1))
        def _():
            send_sketch(2)

        @pl.when((r == 0) & (me == 3))
        def _():
            for k in range(1, NS):
                send_sketch(k)

        @pl.when(r < NS - 1)
        def _():
            relay(r + 1)

        for side in range(2):
            g_copy(r, side).wait_recv()
        for side in range(2):
            work[side, :, :W] = gram_in[r, side].astype(F32) + gram_own[1 - side] + eye
            work[side, :, W:] = eye
        prepare_right(jnp.minimum(r + 1, NS - 1))
        inverse_factors(work, inverse, mixed)

        @pl.when(r < NS - 1)
        def _():
            left_arrives(r + 1)
            prepare_left(r + 1)

        lefted = mm3(inverse[0], mid[...])
        for d in range(D):
            tall[pl.ds(d, W, stride=D), :] = lefted[:, d * W : (d + 1) * W]
        high, low = halves(inverse[1])
        second = jnp.concatenate([high, low, high], axis=1)
        high, low = halves(tall[...])
        fresh = mm_nt(jnp.concatenate([high, high, low], axis=1), second)
        scaling = lax.rsqrt(jnp.mean(fresh * fresh) + 1e-6)
        result = (fresh * scaling).astype(BF16)
        bm[r + 1] = result

        @pl.when(r != me)
        def _():
            o_copy(r).start()

        @pl.when(r == me)
        def _():
            o_stay(r).start()

        @pl.when(r < NS - 1)
        def _():
            sides[0] = result
            high, low = halves(lefted)
            for d in range(D):
                lanes_d = slice(d * W, (d + 1) * W)
                piece = jnp.concatenate([high[:, lanes_d], high[:, lanes_d], low[:, lanes_d]], axis=1)
                tall[pl.ds(d, W, stride=D), :] = mm_nt(second, piece)
            sides[1] = (tall[...] * scaling).astype(BF16)

        return carry

    lax.fori_loop(0, NS, absorb, 0)

    for c in range(CHUNKS):

        @pl.when(me != 0)
        def _():
            r_copy(1, c).wait_send()

        r_copy(2, c).wait_send()
        r_copy(3, c).wait_send()
        for r in range(NS):
            l_copy(r, c).wait_send()
    for k in range(1, NS):
        w_copy(k).wait_send()
    for r in range(NS):
        for side in range(2):
            g_copy(r, side).wait_send()

        @pl.when(r != me)
        def _():
            o_copy(r).wait_send()
            o_arrival(r).wait_recv()

    o_stay(me).wait()


def body(boundary, peps_rows, sketch, ranks, sizes, charges):
    any_space = pl.BlockSpec(memory_space=pl.ANY)
    smem = pl.BlockSpec(memory_space=pltpu.SMEM)
    vmem = pl.BlockSpec(memory_space=pltpu.VMEM)
    dma = pltpu.SemaphoreType.DMA
    result = pl.pallas_call(
        kernel,
        out_shape=jax.ShapeDtypeStruct((NS, W * D, W), BF16),
        in_specs=[vmem, smem, smem, smem, any_space, any_space],
        out_specs=any_space,
        scratch_shapes=[
            pltpu.VMEM((NS, W * D, W), BF16),
            pltpu.VMEM((NS + 1, W * D, W), BF16),
            pltpu.VMEM((2, W * D, W), BF16),
            pltpu.VMEM((NS, W * D, W), BF16),
            pltpu.VMEM((NS, W * D, W), BF16),
            pltpu.VMEM((2, W, W * D), BF16),
            pltpu.VMEM((W, W * D), BF16),
            pltpu.VMEM((64, W), F32),
            pltpu.VMEM((NS, 64, W), BF16),
            pltpu.VMEM((2, 256, 256), BF16),
            pltpu.VMEM((2, W * D, W * D), BF16),
            pltpu.VMEM((W, W * D), F32),
            pltpu.VMEM((W * D, W), F32),
            pltpu.VMEM((2, W, W), F32),
            pltpu.VMEM((NS, 2, W, W), BF16),
            pltpu.VMEM((NS, 2, W, W), BF16),
            pltpu.VMEM((2, W, 2 * W), F32),
            pltpu.VMEM((2, W, W), F32),
            pltpu.VMEM((W, 4 * W), F32),
            dma((NS,)), dma(()), dma((NS - 1, CHUNKS)), dma((NS, CHUNKS)), dma((NS - 1,)),
            dma((NS,)), dma((NS, CHUNKS)), dma((NS, CHUNKS)), dma((NS, 2)), dma((NS, 2)),
            dma((NS,)), dma((NS,)), dma(()),
        ],
        compiler_params=pltpu.CompilerParams(
            collective_id=0, has_side_effects=True, vmem_limit_bytes=56 * 2**20
        ),
        name="absorb_rows",
    )(
        peps_rows.reshape(D * D, D, D),
        ranks.reshape(NS),
        sizes,
        charges,
        boundary.reshape(NS, W * D, W),
        sketch.reshape(NS, W * D, W),
    )
    return result.reshape(1, 1, NS, W, D, W)


def solution(mesh):
    placed = (
        P("col", None, None, None, None),
        P("row", "col", None, None, None, None),
        P("row", "col", None, None, None),
        P("row", "col", None),
        P(),
        P(),
    )
    return jax.shard_map(
        body,
        mesh=mesh,
        in_specs=placed,
        out_specs=P("row", "col", None, None, None, None),
        check_vma=False,
    )
```

time: 94.7 us -> 81.2 us (0.86)
  Pallas kernels: 92 us -> 78.7 us
    pallas_call x1, Pallas kernels: 92 us -> 78.7 us  [body(): pl.pallas_call(kernel, out_shape=jax.ShapeDtypeStruct((NS, W * D, W), BF1...]
where the time goes in v3:
time: 81.2 us; the launch traced here: 81 us
  Pallas kernels  78.7 us (97%)
  local copies, waits for them, and re-layouts  2.26 us (3%)
    pallas_call x1, Pallas kernels, body(): pl.pallas_call(kernel, out_shape=jax.ShapeDtypeStruct((NS, W * D, W), BF1...  78.7 us
    unnamed x1, local copies, waits for them, and re-layouts  2.26 us

profile of v3, /device:TPU:24, one launch (start us, length us, event | category | flops | bytes accessed | tf_op | source)
XLA Modules:
  0.0 81.0 jit_solution(12489419381811725235)
XLA Ops:
  0.0 78.7 %absorb_rows.1 = bf16[4,1024,128]{2,1,0:T(8,128)(2,1)} custom-call(bf16[64,8,8]{2,1,0:T(8,128)(2,1)} %bitcast.8, s32[4]{0:T(128)} %bitcast.9, s32[4]{0:T(128)} %sizes_ref.1, s32[8]{0:T(128)} %charges_ref.1, bf16[4,1024,128]{2,1,0:T(8,128)(2,1)} %bitcast.6, bf16[4,1024,128]{2,1,0:T(8,128)(2,1)} %bitcast.7), custom_call_target="tpu_custom_call" | custom-call | tf_op jit(solution)/shard_map/absorb_rows/pallas_call | solution.py:470
  78.7 2.3 %copy.8 = bf16[1,1,4,128,8,128]{5,4,3,2,1,0:T(8,128)(2,1)} copy(bf16[1,1,4,128,8,128]{5,4,3,2,1,0:T(8,128)(2,1)} %bitcast.5) | data formatting | bytes 2097152

commit v4 on v3

--- a/solution.py
+++ b/solution.py
@@ -9,6 +9,7 @@
 D = 8
 NS = 4
 CHUNKS = 4
+HOPS = 2
 CHUNK = W * D // CHUNKS
 F32 = jnp.float32
 BF16 = jnp.bfloat16
@@ -85,46 +86,35 @@
         a, b = (first[0] + j) % W, (first[1] + j) % W
         return jnp.where(part, vreg(v[:, a : a + 1]), vreg(v[:, b : b + 1]))
 
+    def row(x, i):
+        return vreg(x[i : i + 1, :])
+
+    own = [spread(tiles[0], t) for t in range(8)]
     for q in range(4):
-        columns = [spread(tiles[q], 8 * q + t) for t in range(8)]
-        s = {(i, t): vreg(columns[t][i : i + 1, :]) for t in range(8) for i in range(t, 8)}
         low = {o: [spread(tiles[o], 8 * q + t) for t in range(8)] for o in range(q + 1, 4)}
-        f, n, root = {}, {}, []
+        after = [spread(tiles[q + 1], 8 * q + 8 + t) for t in range(8)] if q < 3 else []
+        pivots = None
         for t in range(8):
-            root.append(lax.rsqrt(s[t, t]))
-            over = root[t] * root[t]
-            for i in range(t + 1, 8):
-                f[i, t] = s[i, t] * over
-                for k in range(t + 1, i + 1):
-                    s[i, k] = s[i, k] - (s[i, t] * s[k, t]) * over
-        for j in range(8):
-            for i in range(j + 1, 8):
-                total = f[i, j]
-                for k in range(j + 1, i):
-                    total = total + f[i, k] * n[k, j]
-                n[i, j] = -total
-        g = {
-            (i, j): (root[i] if i == j else n[i, j] * root[i])
-            for j in range(8)
-            for i in range(j, 8)
-        }
-        panel, result = tiles[q], None
-        for j in range(8):
-            column = jnp.zeros((8, W), F32)
-            for i in range(j, 8):
-                column = jnp.where(sub == i, g[i, j], column)
-            term = column * vreg(panel[j : j + 1, :])
-            result = term if result is None else result + term
-        tiles[q] = result
-        for o in range(q + 1, 4):
-            rest = tiles[o]
-            for t in range(8):
-                factor = None
-                for j in range(t + 1):
-                    term = low[o][j] * g[t, j]
-                    factor = term if factor is None else factor + term
-                rest = rest - factor * vreg(result[t : t + 1, :])
-            tiles[o] = rest
+            pivot = row(own[t], t)
+            over = 1.0 / pivot
+            pivots = pivot if t == 0 else jnp.where(sub == t, pivot, pivots)
+            factor = jnp.where(sub > t, own[t] * over, 0.0)
+            beside = {k: row(own[t], k) for k in range(t + 1, 8)}
+            for k in range(t + 1, 8):
+                own[k] = own[k] - factor * beside[k]
+            here = row(tiles[q], t)
+            for o in range(q + 1, 4):
+                below = low[o][t] * over
+                if o == q + 1:
+                    for k in range(8):
+                        after[k] = after[k] - below * row(low[o][t], k)
+                for k in range(t + 1, 8):
+                    low[o][k] = low[o][k] - below * beside[k]
+                tiles[o] = tiles[o] - below * here
+            if t < 7:
+                tiles[q] = tiles[q] - factor * here
+        tiles[q] = tiles[q] * lax.rsqrt(pivots)
+        own = after
     return tiles
 
 
@@ -158,9 +148,9 @@
 def kernel(
     peps_ref, ranks_ref, sizes_ref, charges_ref, boundary_ref, sketch_ref, out_ref,
     sk, bm, sides, r_raw, l_raw, wides, l_turned, comp32, comp, kron, z, mid, tall,
-    gram_own, gram_out, gram_in, work, inverse, mixed,
+    gram_own, gram_out, gram_in, work, inverse, mixed, hop,
     sk_sem, b_sem, r_send, r_recv, w_send, w_recv, l_send, l_recv,
-    g_send, g_recv, o_send, o_recv, o_local,
+    g_send, g_recv, o_send, o_recv, o_local, hop_recv, hop_send,
 ):
     me = lax.axis_index("row")
     col = lax.axis_index("col")
@@ -230,6 +220,18 @@
 
     def o_stay(r):
         return pltpu.make_async_copy(bm.at[r + 1], out_ref.at[me], o_local)
+
+    def hop_in(c):
+        return pltpu.make_async_remote_copy(
+            src_ref=sk.at[2, chunk(c)], dst_ref=hop.at[c], send_sem=r_send.at[1, c],
+            recv_sem=hop_recv.at[c], device_id=(3, col), device_id_type=MESH,
+        )
+
+    def hop_on(c):
+        return pltpu.make_async_remote_copy(
+            src_ref=hop.at[c], dst_ref=r_raw.at[0, chunk(c)], send_sem=hop_send.at[c],
+            recv_sem=r_recv.at[0, c], device_id=(2, col), device_id_type=MESH,
+        )
 
     def send_sketch(k):
         for c in range(CHUNKS):
@@ -256,7 +258,8 @@
     @pl.when(me == 0)
     def _():
         send_sketch(1)
-        send_sketch(3)
+        for c in range(HOPS):
+            hop_in(c).start()
 
     @pl.when(me == 1)
     def _():
@@ -338,12 +341,6 @@
         gram_out[r, side] = gram.astype(BF16)
         g_copy(r, side).start()
 
-    @pl.when(me == 0)
-    def _():
-        for c in range(CHUNKS):
-            r_copy(1, c).wait_send()
-        send_sketch(2)
-
     size = sizes_ref[me]
     boundary_load.wait()
     start = jnp.where(
@@ -358,8 +355,15 @@
         tall[pl.ds(u, W, stride=D), :] = mid[:, u * W : (u + 1) * W]
     sides[1] = tall[...].astype(BF16)
 
+    @pl.when(me == 3)
+    def _():
+        for c in range(HOPS):
+            hop_in(c).wait_recv()
+            hop_on(c).start()
+
     relay(0)
     prepare_right(0)
+
     eye = (iota((W, W), 0) == iota((W, W), 1)).astype(F32)
 
     def absorb(r, carry):
@@ -368,6 +372,16 @@
 
         @pl.when(r == 0)
         def _():
+            @pl.when(me == 0)
+            def _():
+                for c in range(HOPS):
+                    hop_in(c).wait_send()
+                send_sketch(3)
+                for c in range(CHUNKS):
+                    r_copy(1, c).wait_send()
+                for c in range(HOPS, CHUNKS):
+                    r_copy(2, c).start()
+
             left_arrives(0)
 
             @pl.when(me == 1)
@@ -444,7 +458,18 @@
         def _():
             r_copy(1, c).wait_send()
 
-        r_copy(2, c).wait_send()
+        if c < HOPS:
+
+            @pl.when(me != 0)
+            def _():
+                r_copy(2, c).wait_send()
+
+            @pl.when(me == 3)
+            def _():
+                hop_on(c).wait_send()
+
+        else:
+            r_copy(2, c).wait_send()
         r_copy(3, c).wait_send()
         for r in range(NS):
             l_copy(r, c).wait_send()
@@ -492,9 +517,10 @@
             pltpu.VMEM((2, W, 2 * W), F32),
             pltpu.VMEM((2, W, W), F32),
             pltpu.VMEM((W, 4 * W), F32),
+            pltpu.VMEM((HOPS, CHUNK, W), BF16),
             dma((NS,)), dma(()), dma((NS - 1, CHUNKS)), dma((NS, CHUNKS)), dma((NS - 1,)),
             dma((NS,)), dma((NS, CHUNKS)), dma((NS, CHUNKS)), dma((NS, 2)), dma((NS, 2)),
-            dma((NS,)), dma((NS,)), dma(()),
+            dma((NS,)), dma((NS,)), dma(()), dma((HOPS,)), dma((HOPS,)),
         ],
         compiler_params=pltpu.CompilerParams(
             collective_id=0, has_side_effects=True, vmem_limit_bytes=56 * 2**20

time: 81.2 us -> 75.1 us (0.925)
  Pallas kernels: 78.7 us -> 72.6 us
    pallas_call x1, Pallas kernels: 78.7 us -> 72.6 us  [body(): pl.pallas_call(kernel, out_shape=jax.ShapeDtypeStruct((NS, W * D, W), BF1...]
where the time goes in v4:
time: 75.1 us; the launch traced here: 74.9 us
  Pallas kernels  72.6 us (97%)
  local copies, waits for them, and re-layouts  2.26 us (3%)
    pallas_call x1, Pallas kernels, body(): pl.pallas_call(kernel, out_shape=jax.ShapeDtypeStruct((NS, W * D, W), BF1...  72.6 us
    unnamed x1, local copies, waits for them, and re-layouts  2.26 us

profile of v4, /device:TPU:24, one launch (start us, length us, event | category | flops | bytes accessed | tf_op | source)
XLA Modules:
  0.0 74.9 jit_solution(8760485711807148010)
XLA Ops:
  0.0 72.6 %absorb_rows.1 = bf16[4,1024,128]{2,1,0:T(8,128)(2,1)} custom-call(bf16[64,8,8]{2,1,0:T(8,128)(2,1)} %bitcast.8, s32[4]{0:T(128)} %bitcast.9, s32[4]{0:T(128)} %sizes_ref.1, s32[8]{0:T(128)} %charges_ref.1, bf16[4,1024,128]{2,1,0:T(8,128)(2,1)} %bitcast.6, bf16[4,1024,128]{2,1,0:T(8,128)(2,1)} %bitcast.7), custom_call_target="tpu_custom_call" | custom-call | tf_op jit(solution)/shard_map/absorb_rows/pallas_call | solution.py:495
  72.6 2.3 %copy.8 = bf16[1,1,4,128,8,128]{5,4,3,2,1,0:T(8,128)(2,1)} copy(bf16[1,1,4,128,8,128]{5,4,3,2,1,0:T(8,128)(2,1)} %bitcast.5) | data formatting | bytes 2097152

commit v5 on v4

--- a/solution.py
+++ b/solution.py
@@ -78,9 +78,9 @@
     return jnp.broadcast_to(x, (8, W))
 
 
-def eliminate(tiles, first, part):
+def eliminate(tiles, beyond, first, part):
     sub = iota((8, W), 0)
-    tiles = list(tiles)
+    groups = [list(tiles)] + ([list(beyond)] if beyond else [])
 
     def spread(v, j):
         a, b = (first[0] + j) % W, (first[1] + j) % W
@@ -89,53 +89,87 @@
     def row(x, i):
         return vreg(x[i : i + 1, :])
 
+    tiles = groups[0]
     own = [spread(tiles[0], t) for t in range(8)]
     for q in range(4):
         low = {o: [spread(tiles[o], 8 * q + t) for t in range(8)] for o in range(q + 1, 4)}
         after = [spread(tiles[q + 1], 8 * q + 8 + t) for t in range(8)] if q < 3 else []
         pivots = None
-        for t in range(8):
-            pivot = row(own[t], t)
-            over = 1.0 / pivot
-            pivots = pivot if t == 0 else jnp.where(sub == t, pivot, pivots)
-            factor = jnp.where(sub > t, own[t] * over, 0.0)
-            beside = {k: row(own[t], k) for k in range(t + 1, 8)}
-            for k in range(t + 1, 8):
-                own[k] = own[k] - factor * beside[k]
-            here = row(tiles[q], t)
+        for t in range(0, 8, 2):
+            one, cross, two = row(own[t], t), row(own[t], t + 1), row(own[t + 1], t + 1)
+            determinant = one * two - cross * cross
+            over_one = 1.0 / one
+            over_two = one * (1.0 / determinant)
+            ratio = cross * over_one
+            schur = determinant * over_one
+            pivots = one if t == 0 else jnp.where(sub == t, one, pivots)
+            pivots = jnp.where(sub == t + 1, schur, pivots)
+            rows_one = {k: row(own[t], k) for k in range(t + 2, 8)}
+            rows_two = {k: row(own[t + 1], k) - ratio * rows_one[k] for k in range(t + 2, 8)}
+            factor_one = own[t] * over_one
+            factor_two = (own[t + 1] - own[t] * ratio) * over_two
+            for k in range(t + 2, 8):
+                own[k] = (own[k] - factor_one * rows_one[k]) - factor_two * rows_two[k]
+            factor_one = jnp.where(sub > t, factor_one, 0.0)
+            factor_two = jnp.where(sub > t + 1, factor_two, 0.0)
+            here = []
+            for group in groups:
+                upper = row(group[q], t)
+                here.append((upper, row(group[q], t + 1) - ratio * upper))
             for o in range(q + 1, 4):
-                below = low[o][t] * over
+                second = low[o][t + 1] - low[o][t] * ratio
+                below_one = low[o][t] * over_one
+                below_two = second * over_two
                 if o == q + 1:
                     for k in range(8):
-                        after[k] = after[k] - below * row(low[o][t], k)
-                for k in range(t + 1, 8):
-                    low[o][k] = low[o][k] - below * beside[k]
-                tiles[o] = tiles[o] - below * here
-            if t < 7:
-                tiles[q] = tiles[q] - factor * here
-        tiles[q] = tiles[q] * lax.rsqrt(pivots)
+                        after[k] = (after[k] - below_one * row(low[o][t], k)) - below_two * row(
+                            second, k
+                        )
+                for k in range(t + 2, 8):
+                    low[o][k] = (low[o][k] - below_one * rows_one[k]) - below_two * rows_two[k]
+                for group, (upper, lower) in zip(groups, here):
+                    group[o] = (group[o] - below_one * upper) - below_two * lower
+            for group, (upper, lower) in zip(groups, here):
+                group[q] = (group[q] - factor_one * upper) - factor_two * lower
+        root = lax.rsqrt(pivots)
+        for group in groups:
+            group[q] = group[q] * root
         own = after
-    return tiles
+    return groups
 
 
 def inverse_factors(work, inverse, mixed):
     lane, sub = iota((8, W), 1), iota((8, W), 0)
     group = lane >> 5
+    ready = None
     for k in range(4):
         at = [(k + i) % 4 for i in range(4)]
         part = (group == at[0]) | (group == at[1])
-        tiles = []
+        tiles, beyond = [], []
         for q in range(4):
             rows = pl.ds(32 * k + 8 * q, 8)
-            one = work[0, rows, :W]
-            two = pltpu.roll(work[1, rows, :W], 64, 1)
+            one, two = work[0, rows, :W], pltpu.roll(work[1, rows, :W], 64, 1)
+            if k < 3:
+                beyond.append(jnp.where(group == at[1], one, jnp.where(group == at[3], two, 0.0)))
+            if k > 0:
+                one, two = ready[q]
             unit = ((lane & 31) == (sub + 8 * q)).astype(F32)
             tiles.append(jnp.where(group == at[0], one, jnp.where(group == at[2], two, unit)))
-        done = jnp.concatenate(eliminate(tiles, (32 * k, 32 * k + 64), part), axis=0)
-        mixed[...] = jnp.zeros((W, 4 * W), F32)
-        mixed[pl.ds(32 * at[1], 32), : 2 * W] = work[0, pl.ds(32 * k, 32), :]
-        mixed[pl.ds(32 * at[3], 32), 2 * W :] = work[1, pl.ds(32 * k, 32), :]
-        both = mm3(done, mixed[...])
+        done = eliminate(tiles, beyond, (32 * k, 32 * k + 64), part)
+        if k < 3:
+            ahead = jnp.concatenate(done[1], axis=0)
+            update = mm3_tn(ahead, ahead)
+            ready = []
+            for q in range(4):
+                rows = pl.ds(32 * (k + 1) + 8 * q, 8)
+                one = work[0, rows, :W] - update[32 * at[1] + 8 * q : 32 * at[1] + 8 * q + 8]
+                two = pltpu.roll(work[1, rows, :W], 64, 1)
+                ready.append((one, two - update[32 * at[3] + 8 * q : 32 * at[3] + 8 * q + 8]))
+        slot = k % 2
+        mixed[slot] = jnp.zeros((W, 4 * W), F32)
+        mixed[slot, pl.ds(32 * at[1], 32), : 2 * W] = work[0, pl.ds(32 * k, 32), :]
+        mixed[slot, pl.ds(32 * at[3], 32), 2 * W :] = work[1, pl.ds(32 * k, 32), :]
+        both = mm3(jnp.concatenate(done[0], axis=0), mixed[slot])
         for i in range(2):
             panel = both[:, i * 2 * W : (i + 1) * 2 * W]
             inverse[i, pl.ds(32 * k, 32), :] = panel[:, W:]
@@ -148,9 +182,10 @@
 def kernel(
     peps_ref, ranks_ref, sizes_ref, charges_ref, boundary_ref, sketch_ref, out_ref,
     sk, bm, sides, r_raw, l_raw, wides, l_turned, comp32, comp, kron, z, mid, tall,
-    gram_own, gram_out, gram_in, work, inverse, mixed, hop,
+    gram_own, gram_out, gram_in, work, inverse, mixed, hop, near, near_comp,
     sk_sem, b_sem, r_send, r_recv, w_send, w_recv, l_send, l_recv,
     g_send, g_recv, o_send, o_recv, o_local, hop_recv, hop_send,
+    near_send, near_recv, near_on,
 ):
     me = lax.axis_index("row")
     col = lax.axis_index("col")
@@ -231,6 +266,24 @@
         return pltpu.make_async_remote_copy(
             src_ref=hop.at[c], dst_ref=r_raw.at[0, chunk(c)], send_sem=hop_send.at[c],
             recv_sem=r_recv.at[0, c], device_id=(2, col), device_id_type=MESH,
+        )
+
+    def near_copy():
+        return pltpu.make_async_remote_copy(
+            src_ref=bm.at[0], dst_ref=near, send_sem=near_send.at[0], recv_sem=near_recv.at[0],
+            device_id=(me, left), device_id_type=MESH,
+        )
+
+    def near_comp_copy():
+        return pltpu.make_async_remote_copy(
+            src_ref=comp.at[0], dst_ref=near_comp, send_sem=near_send.at[1],
+            recv_sem=near_recv.at[1], device_id=(me, left), device_id_type=MESH,
+        )
+
+    def near_comp_on(k):
+        return pltpu.make_async_remote_copy(
+            src_ref=near_comp, dst_ref=near_comp, send_sem=near_on.at[k - 1],
+            recv_sem=near_recv.at[1], device_id=(k, col), device_id_type=MESH,
         )
 
     def send_sketch(k):
@@ -271,8 +324,15 @@
         send_sketch(3)
         send_sketch(2)
 
+    boundary_load.wait()
+    near_copy().start()
     compact_tensor(peps_ref, charges_ref, comp32)
     comp[me] = comp32[...].astype(BF16)
+
+    @pl.when(me == 0)
+    def _():
+        near_comp_copy().start()
+
     for k in range(1, NS):
         w_copy(k).start()
 
@@ -296,15 +356,17 @@
         for h in range(D):
             wides[side, :, h * W : (h + 1) * W] = tall[pl.ds(h, W, stride=D), :].astype(BF16)
 
+    def expand(both, slots):
+        turned = pltpu.roll(both, 64, 1)
+        low = iota((64, W), 1) < 64
+        for i, slot in slots:
+            twice = jnp.where(low, both, turned) if i == 0 else jnp.where(low, turned, both)
+            four = jnp.concatenate([twice, twice], axis=1)
+            kron[slot] = jnp.where(block, jnp.concatenate([four] * 4, axis=0), 0.0).astype(BF16)
+
     def prepare_right(r):
         regroup(0, r_raw[r].astype(F32))
-        both = comp[r].astype(F32)
-        turned = pltpu.roll(both, 64, 1)
-        low = iota((64, W), 1) < 64
-        for i, (one, two) in enumerate(((both, turned), (turned, both))):
-            twice = jnp.where(low, one, two)
-            four = jnp.concatenate([twice, twice], axis=1)
-            kron[i] = jnp.where(block, jnp.concatenate([four] * 4, axis=0), 0.0).astype(BF16)
+        expand(comp[r].astype(F32), ((0, 0), (1, 1)))
 
     def prepare_left(r):
         natural = l_raw[r].astype(F32)
@@ -315,8 +377,8 @@
         for c in range(CHUNKS):
             l_copy(r, c).wait_recv()
 
-    def absorb_side(r, side):
-        part = mm(sides[side], wides[side])
+    def absorb_side(lhs, wide, side):
+        part = mm(sides[lhs], wides[wide])
         columns = []
         for q in range(W // 4):
             pieces = [
@@ -325,7 +387,7 @@
                 for h in range(D)
             ]
             columns.append(jnp.concatenate(pieces, axis=0).astype(BF16))
-        whole = mm(kron[side], jnp.concatenate(columns, axis=1))
+        whole = mm(kron[lhs], jnp.concatenate(columns, axis=1))
         for d in range(D):
             pieces = [
                 whole[(i * D + d) * D : (i * D + d + 1) * D, q * W : (q + 1) * W]
@@ -338,22 +400,33 @@
             piece = z[side, :, d * W : (d + 1) * W]
             gram += mm_tn(piece, piece)
         gram_own[side] = gram
-        gram_out[r, side] = gram.astype(BF16)
+
+    def send_gram(r, side):
+        gram_out[r, side] = gram_own[side].astype(BF16)
         g_copy(r, side).start()
 
-    size = sizes_ref[me]
-    boundary_load.wait()
-    start = jnp.where(
-        ((iota((W * D, W), 0) >> 3) < size) & (iota((W * D, W), 1) < size),
-        bm[0].astype(F32), 0.0,
-    )
-    sides[0] = start.astype(BF16)
-    tall[...] = start
-    for u in range(D):
-        mid[:, u * W : (u + 1) * W] = tall[pl.ds(u, W, stride=D), :].T
-    for u in range(D):
-        tall[pl.ds(u, W, stride=D), :] = mid[:, u * W : (u + 1) * W]
-    sides[1] = tall[...].astype(BF16)
+    def masked(block):
+        size = sizes_ref[me]
+        inside = ((iota((W * D, W), 0) >> 3) < size) & (iota((W * D, W), 1) < size)
+        return jnp.where(inside, block.astype(F32), 0.0)
+
+    def turn_side(start, side):
+        tall[...] = start
+        for u in range(D):
+            mid[:, u * W : (u + 1) * W] = tall[pl.ds(u, W, stride=D), :].T
+        for u in range(D):
+            tall[pl.ds(u, W, stride=D), :] = mid[:, u * W : (u + 1) * W]
+        sides[side] = tall[...].astype(BF16)
+
+    def prepare_near():
+        near_copy().wait_recv()
+        turn_side(masked(near[...]), 2)
+
+    sides[0] = masked(bm[0]).astype(BF16)
+
+    @pl.when(me != 0)
+    def _():
+        prepare_near()
 
     @pl.when(me == 3)
     def _():
@@ -367,10 +440,11 @@
     eye = (iota((W, W), 0) == iota((W, W), 1)).astype(F32)
 
     def absorb(r, carry):
-        early = jnp.where(r == 0, 0, 1 - lax.rem(col, 2))
-        absorb_side(r, early)
-
-        @pl.when(r == 0)
+        first_row = r == 0
+        early = jnp.where(first_row, 0, 1 - lax.rem(col, 2))
+        absorb_side(early, early, early)
+
+        @pl.when(first_row)
         def _():
             @pl.when(me == 0)
             def _():
@@ -381,16 +455,43 @@
                     r_copy(1, c).wait_send()
                 for c in range(HOPS, CHUNKS):
                     r_copy(2, c).start()
-
-            left_arrives(0)
+                near_comp_copy().wait_recv()
+                for k in range(1, NS):
+                    near_comp_on(k).start()
+                prepare_near()
+
+            @pl.when(me != 0)
+            def _():
+                near_comp_copy().wait_recv()
+
+            expand(near_comp[...].astype(F32), ((1, 2),))
+
+        @pl.when(jnp.logical_not(first_row))
+        def _():
+            send_gram(r, early)
+
+        absorb_side(
+            jnp.where(first_row, 2, 1 - early), jnp.where(first_row, 0, 1 - early), 1 - early
+        )
+
+        @pl.when(first_row)
+        def _():
+            gram_out[0, 0] = (gram_own[0] + gram_own[1]).astype(BF16)
+            g_copy(0, 0).start()
+            gram_in[0, 1] = gram_own[1].astype(BF16)
+            gram_own[1] = jnp.zeros((W, W), F32)
 
             @pl.when(me == 1)
             def _():
                 send_sketch(1)
 
-            prepare_left(0)
-
-        absorb_side(r, 1 - early)
+            left_arrives(0)
+            l_turned[...] = l_raw[0].astype(F32).T.astype(BF16)
+
+        @pl.when(jnp.logical_not(first_row))
+        def _():
+            send_gram(r, 1 - early)
+
         mid[...] = mm(l_turned[...], z[0])
 
         @pl.when((r == 0) & (me == 1))
@@ -402,22 +503,35 @@
             for k in range(1, NS):
                 send_sketch(k)
 
-        @pl.when(r < NS - 1)
-        def _():
-            relay(r + 1)
-
-        for side in range(2):
-            g_copy(r, side).wait_recv()
+        @pl.when(r == 0)
+        def _():
+            relay(1)
+
+        @pl.when((r > 0) & (r < NS - 1))
+        def _():
+            left_arrives(r + 1)
+            prepare_left(r + 1)
+
+        g_copy(r, 0).wait_recv()
+
+        @pl.when(r > 0)
+        def _():
+            g_copy(r, 1).wait_recv()
+
         for side in range(2):
             work[side, :, :W] = gram_in[r, side].astype(F32) + gram_own[1 - side] + eye
             work[side, :, W:] = eye
         prepare_right(jnp.minimum(r + 1, NS - 1))
         inverse_factors(work, inverse, mixed)
 
-        @pl.when(r < NS - 1)
-        def _():
-            left_arrives(r + 1)
-            prepare_left(r + 1)
+        @pl.when(r < NS - 2)
+        def _():
+            relay(r + 2)
+
+        @pl.when(r == 0)
+        def _():
+            left_arrives(1)
+            prepare_left(1)
 
         lefted = mm3(inverse[0], mid[...])
         for d in range(D):
@@ -475,9 +589,18 @@
             l_copy(r, c).wait_send()
     for k in range(1, NS):
         w_copy(k).wait_send()
+    near_copy().wait_send()
+
+    @pl.when(me == 0)
+    def _():
+        near_comp_copy().wait_send()
+        for k in range(1, NS):
+            near_comp_on(k).wait_send()
+
     for r in range(NS):
-        for side in range(2):
-            g_copy(r, side).wait_send()
+        g_copy(r, 0).wait_send()
+        if r > 0:
+            g_copy(r, 1).wait_send()
 
         @pl.when(r != me)
         def _():
@@ -500,14 +623,14 @@
         scratch_shapes=[
             pltpu.VMEM((NS, W * D, W), BF16),
             pltpu.VMEM((NS + 1, W * D, W), BF16),
-            pltpu.VMEM((2, W * D, W), BF16),
+            pltpu.VMEM((3, W * D, W), BF16),
             pltpu.VMEM((NS, W * D, W), BF16),
             pltpu.VMEM((NS, W * D, W), BF16),
             pltpu.VMEM((2, W, W * D), BF16),
             pltpu.VMEM((W, W * D), BF16),
             pltpu.VMEM((64, W), F32),
             pltpu.VMEM((NS, 64, W), BF16),
-            pltpu.VMEM((2, 256, 256), BF16),
+            pltpu.VMEM((3, 256, 256), BF16),
             pltpu.VMEM((2, W * D, W * D), BF16),
             pltpu.VMEM((W, W * D), F32),
             pltpu.VMEM((W * D, W), F32),
@@ -516,11 +639,14 @@
             pltpu.VMEM((NS, 2, W, W), BF16),
             pltpu.VMEM((2, W, 2 * W), F32),
             pltpu.VMEM((2, W, W), F32),
-            pltpu.VMEM((W, 4 * W), F32),
+            pltpu.VMEM((2, W, 4 * W), F32),
             pltpu.VMEM((HOPS, CHUNK, W), BF16),
+            pltpu.VMEM((W * D, W), BF16),
+            pltpu.VMEM((64, W), BF16),
             dma((NS,)), dma(()), dma((NS - 1, CHUNKS)), dma((NS, CHUNKS)), dma((NS - 1,)),
             dma((NS,)), dma((NS, CHUNKS)), dma((NS, CHUNKS)), dma((NS, 2)), dma((NS, 2)),
             dma((NS,)), dma((NS,)), dma(()), dma((HOPS,)), dma((HOPS,)),
+            dma((2,)), dma((2,)), dma((NS - 1,)),
         ],
         compiler_params=pltpu.CompilerParams(
             collective_id=0, has_side_effects=True, vmem_limit_bytes=56 * 2**20

time: 75.1 us -> 70.9 us (0.944)
  Pallas kernels: 72.6 us -> 68.3 us
    pallas_call x1, Pallas kernels: 72.6 us -> 68.3 us  [body(): pl.pallas_call(kernel, out_shape=jax.ShapeDtypeStruct((NS, W * D, W), BF1...]
where the time goes in v5:
time: 70.9 us; the launch traced here: 70.6 us
  Pallas kernels  68.3 us (96%)
  local copies, waits for them, and re-layouts  2.26 us (3%)
    pallas_call x1, Pallas kernels, body(): pl.pallas_call(kernel, out_shape=jax.ShapeDtypeStruct((NS, W * D, W), BF1...  68.3 us
    unnamed x1, local copies, waits for them, and re-layouts  2.26 us

profile of v5, /device:TPU:24, one launch (start us, length us, event | category | flops | bytes accessed | tf_op | source)
XLA Modules:
  0.0 70.6 jit_solution(12279165720626807383)
XLA Ops:
  0.0 68.3 %absorb_rows.1 = bf16[4,1024,128]{2,1,0:T(8,128)(2,1)} custom-call(bf16[64,8,8]{2,1,0:T(8,128)(2,1)} %bitcast.8, s32[4]{0:T(128)} %bitcast.9, s32[4]{0:T(128)} %sizes_ref.1, s32[8]{0:T(128)} %charges_ref.1, bf16[4,1024,128]{2,1,0:T(8,128)(2,1)} %bitcast.6, bf16[4,1024,128]{2,1,0:T(8,128)(2,1)} %bitcast.7), custom_call_target="tpu_custom_call" | custom-call | tf_op jit(solution)/shard_map/absorb_rows/pallas_call | solution.py:618
  68.3 2.3 %copy.8 = bf16[1,1,4,128,8,128]{5,4,3,2,1,0:T(8,128)(2,1)} copy(bf16[1,1,4,128,8,128]{5,4,3,2,1,0:T(8,128)(2,1)} %bitcast.5) | data formatting | bytes 2097152

commit v6 on v5

--- a/solution.py
+++ b/solution.py
@@ -182,7 +182,7 @@
 def kernel(
     peps_ref, ranks_ref, sizes_ref, charges_ref, boundary_ref, sketch_ref, out_ref,
     sk, bm, sides, r_raw, l_raw, wides, l_turned, comp32, comp, kron, z, mid, tall,
-    gram_own, gram_out, gram_in, work, inverse, mixed, hop, near, near_comp,
+    gram_own, gram_out, gram_in, work, inverse, mixed, hop, near, near_comp, turned,
     sk_sem, b_sem, r_send, r_recv, w_send, w_recv, l_send, l_recv,
     g_send, g_recv, o_send, o_recv, o_local, hop_recv, hop_send,
     near_send, near_recv, near_on,
@@ -286,6 +286,15 @@
             recv_sem=near_recv.at[1], device_id=(k, col), device_id_type=MESH,
         )
 
+    def send_result(r):
+        @pl.when(r != me)
+        def _():
+            o_copy(r).start()
+
+        @pl.when(r == me)
+        def _():
+            o_stay(r).start()
+
     def send_sketch(k):
         for c in range(CHUNKS):
             r_copy(k, c).start()
@@ -297,15 +306,19 @@
         )
     for c in (left, right):
         pl.semaphore_signal(barrier, inc=1, device_id=(me, c), device_id_type=MESH)
-    for s in range(NS):
+    away = [lax.rem(me + k, NS) for k in (1, 2, 3, 0)]
+    for s in away:
         sketch_load(s).start()
     boundary_load = pltpu.make_async_copy(boundary_ref.at[me], bm.at[0], b_sem)
     boundary_load.start()
     lanes = iota((1, W), 1)
-    for s in range(NS):
+
+    def mask_sketch(s):
         sketch_load(s).wait()
         sk[s] = sk[s] * (lanes < ranks_ref[s]).astype(BF16)
-    r_raw[me] = sk[me]
+
+    mask_sketch(away[0])
+    mask_sketch(away[1])
     pl.semaphore_wait(barrier, NS + 1)
 
     @pl.when(me == 0)
@@ -314,6 +327,10 @@
         for c in range(HOPS):
             hop_in(c).start()
 
+    mask_sketch(away[2])
+    mask_sketch(away[3])
+    r_raw[me] = sk[me]
+
     @pl.when(me == 1)
     def _():
         send_sketch(3)
@@ -357,10 +374,10 @@
             wides[side, :, h * W : (h + 1) * W] = tall[pl.ds(h, W, stride=D), :].astype(BF16)
 
     def expand(both, slots):
-        turned = pltpu.roll(both, 64, 1)
+        rolled = pltpu.roll(both, 64, 1)
         low = iota((64, W), 1) < 64
         for i, slot in slots:
-            twice = jnp.where(low, both, turned) if i == 0 else jnp.where(low, turned, both)
+            twice = jnp.where(low, both, rolled) if i == 0 else jnp.where(low, rolled, both)
             four = jnp.concatenate([twice, twice], axis=1)
             kron[slot] = jnp.where(block, jnp.concatenate([four] * 4, axis=0), 0.0).astype(BF16)
 
@@ -533,34 +550,35 @@
             left_arrives(1)
             prepare_left(1)
 
-        lefted = mm3(inverse[0], mid[...])
-        for d in range(D):
-            tall[pl.ds(d, W, stride=D), :] = lefted[:, d * W : (d + 1) * W]
-        high, low = halves(inverse[1])
-        second = jnp.concatenate([high, low, high], axis=1)
-        high, low = halves(tall[...])
-        fresh = mm_nt(jnp.concatenate([high, high, low], axis=1), second)
-        scaling = lax.rsqrt(jnp.mean(fresh * fresh) + 1e-6)
-        result = (fresh * scaling).astype(BF16)
-        bm[r + 1] = result
-
-        @pl.when(r != me)
-        def _():
-            o_copy(r).start()
-
-        @pl.when(r == me)
-        def _():
-            o_stay(r).start()
+        def solved():
+            lefted = mm3(inverse[0], mid[...])
+            for d in range(D):
+                tall[pl.ds(d, W, stride=D), :] = lefted[:, d * W : (d + 1) * W]
+            high, low = halves(inverse[1])
+            second = jnp.concatenate([high, low, high], axis=1)
+            high, low = halves(tall[...])
+            fresh = mm_nt(jnp.concatenate([high, high, low], axis=1), second)
+            return lefted, second, fresh, lax.rsqrt(jnp.mean(fresh * fresh) + 1e-6)
 
         @pl.when(r < NS - 1)
         def _():
-            sides[0] = result
+            lefted, second, fresh, scaling = solved()
             high, low = halves(lefted)
             for d in range(D):
                 lanes_d = slice(d * W, (d + 1) * W)
                 piece = jnp.concatenate([high[:, lanes_d], high[:, lanes_d], low[:, lanes_d]], axis=1)
-                tall[pl.ds(d, W, stride=D), :] = mm_nt(second, piece)
-            sides[1] = (tall[...] * scaling).astype(BF16)
+                turned[pl.ds(d, W, stride=D), :] = mm_nt(second, piece)
+            result = (fresh * scaling).astype(BF16)
+            sides[0] = result
+            bm[r + 1] = result
+            sides[1] = (turned[...] * scaling).astype(BF16)
+            send_result(r)
+
+        @pl.when(r == NS - 1)
+        def _():
+            _, _, fresh, scaling = solved()
+            bm[r + 1] = (fresh * scaling).astype(BF16)
+            send_result(r)
 
         return carry
 
@@ -617,7 +635,7 @@
     dma = pltpu.SemaphoreType.DMA
     result = pl.pallas_call(
         kernel,
-        out_shape=jax.ShapeDtypeStruct((NS, W * D, W), BF16),
+        out_shape=pltpu.VMEM((NS, W * D, W), BF16),
         in_specs=[vmem, smem, smem, smem, any_space, any_space],
         out_specs=any_space,
         scratch_shapes=[
@@ -643,6 +661,7 @@
             pltpu.VMEM((HOPS, CHUNK, W), BF16),
             pltpu.VMEM((W * D, W), BF16),
             pltpu.VMEM((64, W), BF16),
+            pltpu.VMEM((W * D, W), F32),
             dma((NS,)), dma(()), dma((NS - 1, CHUNKS)), dma((NS, CHUNKS)), dma((NS - 1,)),
             dma((NS,)), dma((NS, CHUNKS)), dma((NS, CHUNKS)), dma((NS, 2)), dma((NS, 2)),
             dma((NS,)), dma((NS,)), dma(()), dma((HOPS,)), dma((HOPS,)),

time: 70.9 us -> 68.1 us (0.961)
  Pallas kernels: 68.3 us -> 66.9 us
  local copies, waits for them, and re-layouts: 2.26 us -> 0.97 us
    pallas_call x1, Pallas kernels: 68.3 us -> 66.9 us  [body(): pl.pallas_call(kernel, out_shape=pltpu.VMEM((NS, W * D, W), BF16), in_spe...]
    unnamed x1, local copies, waits for them, and re-layouts: 2.26 us -> 0.97 us
where the time goes in v6:
time: 68.1 us; the launch traced here: 67.9 us
  Pallas kernels  66.9 us (98%)
  local copies, waits for them, and re-layouts  0.97 us (1%)
    pallas_call x1, Pallas kernels, body(): pl.pallas_call(kernel, out_shape=pltpu.VMEM((NS, W * D, W), BF16), in_spe...  66.9 us

profile of v6, /device:TPU:24, one launch (start us, length us, event | category | flops | bytes accessed | tf_op | source)
XLA Modules:
  0.0 67.9 jit_solution(16696747323460855667)
XLA Ops:
  0.0 66.9 %absorb_rows.1 = bf16[4,1024,128]{2,1,0:T(8,128)(2,1)S(1)} custom-call(bf16[64,8,8]{2,1,0:T(8,128)(2,1)} %bitcast.8, s32[4]{0:T(128)} %bitcast.9, s32[4]{0:T(128)} %sizes_ref.1, s32[8]{0:T(128)} %charges_ref.1, bf16[4,1024,128]{2,1,0:T(8,128)(2,1)} %bitcast.6, bf16[4,1024,128]{2,1,0:T(8,128)(2,1)} %bitcast.7), custom_call_target="tpu_custom_call" | custom-call | tf_op jit(solution)/shard_map/absorb_rows/pallas_call | solution.py:636
  67.0 1.0 %copy.8 = bf16[1,1,4,128,8,128]{5,4,3,2,1,0:T(8,128)(2,1)} copy(bf16[1,1,4,128,8,128]{5,4,3,2,1,0:T(8,128)(2,1)S(1)} %bitcast.5) | data formatting | bytes 2097152

commit v7 on v6

--- a/solution.py
+++ b/solution.py
@@ -454,6 +454,10 @@
     relay(0)
     prepare_right(0)
 
+    @pl.when(me == 1)
+    def _():
+        send_sketch(1)
+
     eye = (iota((W, W), 0) == iota((W, W), 1)).astype(F32)
 
     def absorb(r, carry):
@@ -498,10 +502,6 @@
             gram_in[0, 1] = gram_own[1].astype(BF16)
             gram_own[1] = jnp.zeros((W, W), F32)
 
-            @pl.when(me == 1)
-            def _():
-                send_sketch(1)
-
             left_arrives(0)
             l_turned[...] = l_raw[0].astype(F32).T.astype(BF16)
 
@@ -523,11 +523,13 @@
         @pl.when(r == 0)
         def _():
             relay(1)
+            prepare_right(1)
 
         @pl.when((r > 0) & (r < NS - 1))
         def _():
             left_arrives(r + 1)
             prepare_left(r + 1)
+            prepare_right(r + 1)
 
         g_copy(r, 0).wait_recv()
 
@@ -538,7 +540,6 @@
         for side in range(2):
             work[side, :, :W] = gram_in[r, side].astype(F32) + gram_own[1 - side] + eye
             work[side, :, W:] = eye
-        prepare_right(jnp.minimum(r + 1, NS - 1))
         inverse_factors(work, inverse, mixed)
 
         @pl.when(r < NS - 2)

time: 68.1 us -> 67.9 us (level)
  no operation moved by 1% of the time
where the time goes in v7:
time: 67.9 us; the launch traced here: 67.7 us
  Pallas kernels  66.7 us (98%)
  local copies, waits for them, and re-layouts  0.97 us (1%)
    pallas_call x1, Pallas kernels, body(): pl.pallas_call(kernel, out_shape=pltpu.VMEM((NS, W * D, W), BF16), in_spe...  66.7 us

profile of v7, /device:TPU:24, one launch (start us, length us, event | category | flops | bytes accessed | tf_op | source)
XLA Modules:
  0.0 67.7 jit_solution(15955014767081368816)
XLA Ops:
  0.0 66.7 %absorb_rows.1 = bf16[4,1024,128]{2,1,0:T(8,128)(2,1)S(1)} custom-call(bf16[64,8,8]{2,1,0:T(8,128)(2,1)} %bitcast.8, s32[4]{0:T(128)} %bitcast.9, s32[4]{0:T(128)} %sizes_ref.1, s32[8]{0:T(128)} %charges_ref.1, bf16[4,1024,128]{2,1,0:T(8,128)(2,1)} %bitcast.6, bf16[4,1024,128]{2,1,0:T(8,128)(2,1)} %bitcast.7), custom_call_target="tpu_custom_call" | custom-call | tf_op jit(solution)/shard_map/absorb_rows/pallas_call | solution.py:637
  66.7 1.0 %copy.8 = bf16[1,1,4,128,8,128]{5,4,3,2,1,0:T(8,128)(2,1)} copy(bf16[1,1,4,128,8,128]{5,4,3,2,1,0:T(8,128)(2,1)S(1)} %bitcast.5) | data formatting | bytes 2097152

commit v8 on v7

--- a/solution.py
+++ b/solution.py
@@ -8,8 +8,8 @@
 W = 128
 D = 8
 NS = 4
-CHUNKS = 4
-HOPS = 2
+CHUNKS = 2
+HOPS = 1
 CHUNK = W * D // CHUNKS
 F32 = jnp.float32
 BF16 = jnp.bfloat16

time: 67.9 us -> 67.6 us (level)
  no operation moved by 1% of the time
where the time goes in v8:
time: 67.6 us; the launch traced here: 67.5 us
  Pallas kernels  66.5 us (98%)
  local copies, waits for them, and re-layouts  0.97 us (1%)
    pallas_call x1, Pallas kernels, body(): pl.pallas_call(kernel, out_shape=pltpu.VMEM((NS, W * D, W), BF16), in_spe...  66.5 us

profile of v8, /device:TPU:24, one launch (start us, length us, event | category | flops | bytes accessed | tf_op | source)
XLA Modules:
  0.0 67.5 jit_solution(1945311358127450136)
XLA Ops:
  0.0 66.5 %absorb_rows.1 = bf16[4,1024,128]{2,1,0:T(8,128)(2,1)S(1)} custom-call(bf16[64,8,8]{2,1,0:T(8,128)(2,1)} %bitcast.8, s32[4]{0:T(128)} %bitcast.9, s32[4]{0:T(128)} %sizes_ref.1, s32[8]{0:T(128)} %charges_ref.1, bf16[4,1024,128]{2,1,0:T(8,128)(2,1)} %bitcast.6, bf16[4,1024,128]{2,1,0:T(8,128)(2,1)} %bitcast.7), custom_call_target="tpu_custom_call" | custom-call | tf_op jit(solution)/shard_map/absorb_rows/pallas_call | solution.py:637
  66.5 1.0 %copy.8 = bf16[1,1,4,128,8,128]{5,4,3,2,1,0:T(8,128)(2,1)} copy(bf16[1,1,4,128,8,128]{5,4,3,2,1,0:T(8,128)(2,1)S(1)} %bitcast.5) | data formatting | bytes 2097152
